TPU v7x, 32 devices: a whole 2x2x4 slice. The times are simulated.
32 devices in a mesh: box: 4 (over z), slab: 8 (over y, x, core).
Axes of the slice: x: 2, y: 2, z: 4, core: 2. Of those that a mesh axis runs over, the one named last changes fastest.
Arguments:
- hidden_field: bfloat16 [4, 8, 64, 128, 128], P('box', None, 'slab'), may hold values from -6 to 6
- cone_grad: float32 [256, 128, 128], P(('box', 'slab')), may hold values from -6 to 6
- conv_weight: bfloat16 [8, 27], replicated, may hold values from -0.4375 to 0.4375
- box_lower: int32 [256], P(('box', 'slab')), may hold values from 0 to 3, as said below
- box_upper: int32 [256], P(('box', 'slab')), may hold values from 0 to 3, as said below
- plane_lower: int32 [256], P(('box', 'slab')), may hold values from 0 to 63, as said below
- plane_upper: int32 [256], P(('box', 'slab')), may hold values from 0 to 63, as said below
- weight_lower: int32 [256], P(('box', 'slab')), may hold values from 0 to 256
- weight_upper: int32 [256], P(('box', 'slab')), may hold values from 0 to 256, as said below
Outputs:
- hidden_grad: bfloat16 [4, 8, 64, 128, 128], P('box', None, 'slab')
- weight_grad: float32 [8, 27], replicated
Inputs may be any that keep to these rules, and one draw needn't show every extreme that they name: With g = l // 64 the group of plane l, box_lower[l] is g or g - 1 (never below 0). box_upper[l] = min(box_lower[l] + 1, 3). Each box b has one offset o_b, and for one box, drawn from the seed, o_b = 32; plane_lower[l] = (l + o_b) mod 64 with b = box_lower[l]. plane_upper[l] = (l + o_b) mod 64 with b = box_upper[l], the same offsets. weight_upper[l] = 256 - weight_lower[l].
All inputs are finite; a program needn't handle non-finite values.
Results may differ from a plain program's by a relative error of at most 0.005.
Values may be sent and summed in bfloat16 or wider, within the bound.
A program may use at most 320 MiB of HBM per device.

v0:
```python
import functools
import math

import jax
import jax.numpy as jnp
from jax import lax
from jax.experimental import pallas as pl
from jax.experimental.pallas import tpu as pltpu
from jax.sharding import PartitionSpec as P

WDEN = 256
MESH = pl.DeviceIdType.MESH
F32 = jnp.float32
BF16 = jnp.bfloat16
TAP_ROWS = 32


def kernel(
    nbox,
    nslab,
    scale,
    bl_hbm,
    bu_hbm,
    plo_hbm,
    pup_hbm,
    wl_hbm,
    wu_hbm,
    cone_hbm,
    weight_hbm,
    h_hbm,
    out,
    wg,
    bl,
    bu,
    plo,
    pup,
    wl,
    wu,
    cone,
    weight,
    hbuf,
    own,
    z_up,
    z_dn,
    from_above,
    from_below,
    send_a,
    recv_a,
    send_b,
    recv_b,
    ht,
    wmat,
    wide,
    lmat,
    part,
    msg,
    slab_terms,
    msg2,
    box_terms,
    isem,
    hsem,
    up_s,
    up_r,
    dn_s,
    dn_r,
    a_s,
    a_r,
    b_s,
    b_r,
    c_s,
    c_r,
    d_s,
    d_r,
):
    g = lax.axis_index("box")
    me = lax.axis_index("slab")
    depth, nx, ny = cone.shape
    rows = nx // nslab
    nz = depth * nslab
    ch = hbuf.shape[0]
    pairs = ch // 2

    loads = [
        pltpu.make_async_copy(source, held, isem.at[i])
        for i, (source, held) in enumerate(
            (
                (cone_hbm, cone),
                (bl_hbm, bl),
                (bu_hbm, bu),
                (wl_hbm, wl),
                (wu_hbm, wu),
                (plo_hbm, plo),
                (pup_hbm, pup),
                (weight_hbm, weight),
            )
        )
    ]
    for load in loads:
        load.start()
    h_copy = pltpu.make_async_copy(h_hbm, hbuf, hsem)
    h_copy.start()

    barrier = pltpu.get_barrier_semaphore()

    def greet_slab(j, _):
        pl.semaphore_signal(barrier, inc=1, device_id={"slab": lax.rem(me + j, nslab)}, device_id_type=MESH)
        return 0

    def greet_box(j, _):
        pl.semaphore_signal(barrier, inc=1, device_id={"box": lax.rem(g + j, nbox)}, device_id_type=MESH)
        return 0

    lax.fori_loop(1, nslab, greet_slab, 0)
    lax.fori_loop(1, nbox, greet_box, 0)

    for load in loads:
        load.wait()

    def weigh(i, _):
        lower = wl[i].astype(F32) * (1.0 / WDEN)
        upper = wu[i].astype(F32) * (1.0 / WDEN)
        own_c = jnp.where(bl[i] == g, lower, 0.0) + jnp.where(bu[i] == g, upper, 0.0)
        below_c = jnp.where(bl[i] == g - 1, lower, 0.0)
        above_c = jnp.where(bu[i] == g + 1, upper, 0.0)
        plane = cone[i].reshape(nslab, rows, ny)
        z_up[:, i] = (above_c * plane).astype(z_up.dtype)
        z_dn[:, i] = (below_c * plane).astype(z_dn.dtype)
        own[:, i] = own_c * plane
        return 0

    lax.fori_loop(0, depth, weigh, 0)
    pl.semaphore_wait(barrier, nslab - 1 + nbox - 1)

    def up_copy(t):
        return pltpu.make_async_remote_copy(
            src_ref=z_up.at[t],
            dst_ref=from_below.at[t],
            send_sem=up_s.at[t],
            recv_sem=up_r.at[t],
            device_id={"box": lax.rem(g + 1, nbox)},
            device_id_type=MESH,
        )

    def dn_copy(t):
        return pltpu.make_async_remote_copy(
            src_ref=z_dn.at[t],
            dst_ref=from_above.at[t],
            send_sem=dn_s.at[t],
            recv_sem=dn_r.at[t],
            device_id={"box": lax.rem(g + nbox - 1, nbox)},
            device_id_type=MESH,
        )

    def send_z(j, _):
        t = lax.rem(me + 1 + j, nslab)

        @pl.when(g < nbox - 1)
        def _():
            up_copy(t).start()

        @pl.when(g > 0)
        def _():
            dn_copy(t).start()

        return 0

    lax.fori_loop(0, nslab, send_z, 0)

    h_copy.wait()

    def turn(c, _):
        for z in range(depth):
            ht[pl.ds(pl.multiple_of(c * ny, ny), ny), z * nx : (z + 1) * nx] = hbuf[c, z].T
        return 0

    lax.fori_loop(0, ch, turn, 0)

    def merge(t):
        @pl.when(g < nbox - 1)
        def _():
            dn_copy(t).wait_recv()
            own[t] = own[t] + from_above[t].astype(F32)

        @pl.when(g > 0)
        def _():
            up_copy(t).wait_recv()
            own[t] = own[t] + from_below[t].astype(F32)

    def a_copy(t, source):
        return pltpu.make_async_remote_copy(
            src_ref=send_a.at[t],
            dst_ref=recv_a.at[pl.ds(source * depth, depth)],
            send_sem=a_s.at[t],
            recv_sem=a_r.at[source],
            device_id={"slab": t},
            device_id_type=MESH,
        )

    def merge_send(j, _):
        t = lax.rem(me + 1 + j, nslab)
        merge(t)
        send_a[t] = own[t].astype(BF16)
        a_copy(t, me).start()
        return 0

    lax.fori_loop(0, nslab - 1, merge_send, 0)
    merge(me)
    recv_a[pl.ds(me * depth, depth)] = own[me].astype(BF16)

    y_in = lax.broadcasted_iota(jnp.int32, (ny, ny), 0)
    y_out = lax.broadcasted_iota(jnp.int32, (ny, ny), 1)
    hits = [y_in == lax.rem(y_out - dy + ny, ny) for dy in (-1, 0, 1)]
    taps = weight[...].astype(F32)
    for k in range(27):
        wide[k] = jnp.broadcast_to(taps[:, k : k + 1], (ch, ny))

    def fill(p, _):
        for cc in range(2):
            for j in range(9):
                block = jnp.zeros((ny, ny), F32)
                for d in range(3):
                    block = jnp.where(hits[d], wide[3 * j + d, pl.ds(2 * p + cc, 1)], block)
                wmat[p, j * ny : (j + 1) * ny, cc * ny : (cc + 1) * ny] = block.astype(BF16)
        return 0

    lax.fori_loop(0, pairs, fill, 0)

    def wait_a(j, _):
        source = lax.rem(me + j, nslab)
        a_copy(source, source).wait_recv()
        return 0

    lax.fori_loop(1, nslab, wait_a, 0)

    offset = jnp.where(bl[0] == g, plo[0], pup[0]) - me * depth

    def wanted(s, q):
        return recv_a[lax.rem(s * depth - 1 + q - offset + 2 * nz, nz)]

    def b_copy(s, source):
        return pltpu.make_async_remote_copy(
            src_ref=send_b.at[s],
            dst_ref=recv_b.at[source],
            send_sem=b_s.at[s],
            recv_sem=b_r.at[source],
            device_id={"slab": s},
            device_id_type=MESH,
        )

    def turn_send(j, _):
        s = lax.rem(me + 1 + j, nslab)
        for q in range(depth + 2):
            send_b[s, q] = wanted(s, q)
        b_copy(s, me).start()
        return 0

    lax.fori_loop(0, nslab - 1, turn_send, 0)
    for q in range(depth + 2):
        recv_b[me, q] = wanted(me, q)

    def wait_b(j, _):
        source = lax.rem(me + j, nslab)
        b_copy(source, source).wait_recv()
        return 0

    lax.fori_loop(1, nslab, wait_b, 0)

    for q in range(depth + 2):
        plane = recv_b[:, q].astype(F32).reshape(nx, ny)
        for dx in (-1, 0, 1):
            moved = (plane if dx == 0 else pltpu.roll(plane, dx % nx, 0)).astype(BF16)
            for dz in (-1, 0, 1):
                z, j = q + dz - 1, (dz + 1) * 3 + dx + 1
                if 0 <= z < depth:
                    lmat[z * nx : (z + 1) * nx, j * ny : (j + 1) * ny] = moved

    part[...] = jnp.zeros_like(part)
    picks = [y_out == lax.rem(y_in - dy + ny, ny) for dy in (-1, 0, 1)]

    def pair_terms(p, _):
        prod = jnp.dot(
            ht[pl.ds(pl.multiple_of(p * 2 * ny, 2 * ny), 2 * ny), :], lmat[...], preferred_element_type=F32
        )
        for cc in range(2):
            for j in range(9):
                block = prod[cc * ny : (cc + 1) * ny, j * ny : (j + 1) * ny]
                for d in range(3):
                    row = cc * TAP_ROWS + 3 * j + d
                    part[p, row : row + 1] = jnp.sum(jnp.where(picks[d], block, 0.0), axis=0, keepdims=True)
        return 0

    lax.fori_loop(0, pairs, pair_terms, 0)
    msg[...] = jnp.zeros_like(msg)
    for half in range(pairs // 2):
        both = part[2 * half : 2 * half + 2].reshape(4 * TAP_ROWS, ny)
        msg[half : half + 1] = jnp.sum(both.T, axis=0, keepdims=True)

    def c_copy(s, source):
        return pltpu.make_async_remote_copy(
            src_ref=msg,
            dst_ref=slab_terms.at[source],
            send_sem=c_s.at[s],
            recv_sem=c_r.at[source],
            device_id={"slab": s},
            device_id_type=MESH,
        )

    def d_copy(b, source):
        return pltpu.make_async_remote_copy(
            src_ref=msg2,
            dst_ref=box_terms.at[source],
            send_sem=d_s.at[b],
            recv_sem=d_r.at[source],
            device_id={"box": b},
            device_id_type=MESH,
        )

    def send_c(j, _):
        c_copy(lax.rem(me + j, nslab), me).start()
        return 0

    def send_d(j, _):
        d_copy(lax.rem(g + j, nbox), g).start()
        return 0

    def wait_c(j, _):
        source = lax.rem(me + j, nslab)
        c_copy(source, source).wait_recv()
        return 0

    def wait_d(j, _):
        source = lax.rem(g + j, nbox)
        d_copy(source, source).wait_recv()
        return 0

    def pair_grads(p, _):
        grads = jnp.dot(lmat[...], wmat[p], preferred_element_type=F32)
        for cc in range(2):
            out[2 * p + cc] = grads[:, cc * ny : (cc + 1) * ny].reshape(depth, nx, ny).astype(BF16)
        return 0

    slab_terms[me] = msg[...]
    lax.fori_loop(1, nslab, send_c, 0)
    lax.fori_loop(0, pairs // 2, pair_grads, 0)
    lax.fori_loop(1, nslab, wait_c, 0)
    total = slab_terms[0]
    for s in range(1, nslab):
        total = total + slab_terms[s]
    msg2[...] = total
    box_terms[g] = total
    lax.fori_loop(1, nbox, send_d, 0)
    lax.fori_loop(pairs // 2, pairs, pair_grads, 0)
    lax.fori_loop(1, nbox, wait_d, 0)
    total = box_terms[0]
    for b in range(1, nbox):
        total = total + box_terms[b]
    total = total * scale
    for c in range(ch):
        at = (c % 4) * TAP_ROWS
        wg[c : c + 1, :] = total[c // 4 : c // 4 + 1, at : at + 27]

    def drain_z(t, _):
        @pl.when(g < nbox - 1)
        def _():
            up_copy(t).wait_send()

        @pl.when(g > 0)
        def _():
            dn_copy(t).wait_send()

        return 0

    def drain_slab(j, _):
        s = lax.rem(me + j, nslab)
        a_copy(s, me).wait_send()
        b_copy(s, me).wait_send()
        c_copy(s, me).wait_send()
        return 0

    def drain_box(j, _):
        d_copy(lax.rem(g + j, nbox), g).wait_send()
        return 0

    lax.fori_loop(0, nslab, drain_z, 0)
    lax.fori_loop(1, nslab, drain_slab, 0)
    lax.fori_loop(1, nbox, drain_box, 0)


def local(
    nbox,
    nslab,
    hidden_field,
    cone_grad,
    conv_weight,
    box_lower,
    box_upper,
    plane_lower,
    plane_upper,
    weight_lower,
    weight_upper,
):
    _, ch, depth, nx, ny = hidden_field.shape
    rows = nx // nslab
    nz = depth * nslab
    scale = 1.0 / math.sqrt(nbox * nz * nx * ny)
    vmem = pl.BlockSpec(memory_space=pltpu.VMEM)
    hbm = pl.BlockSpec(memory_space=pltpu.HBM)
    dma = pltpu.SemaphoreType.DMA
    link = BF16
    hidden_grad, weight_grad = pl.pallas_call(
        functools.partial(kernel, nbox, nslab, scale),
        out_shape=(
            pltpu.VMEM((ch, depth, nx, ny), BF16),
            jax.ShapeDtypeStruct((ch, 27), F32),
        ),
        in_specs=[hbm] * 9,
        out_specs=(vmem, vmem),
        scratch_shapes=[
            *[pltpu.SMEM((depth,), jnp.int32)] * 6,
            pltpu.VMEM(cone_grad.shape, F32),
            pltpu.VMEM(conv_weight.shape, BF16),
            pltpu.VMEM((ch, depth, nx, ny), BF16),
            pltpu.VMEM((nslab, depth, rows, ny), F32),
            pltpu.VMEM((nslab, depth, rows, ny), link),
            pltpu.VMEM((nslab, depth, rows, ny), link),
            pltpu.VMEM((nslab, depth, rows, ny), link),
            pltpu.VMEM((nslab, depth, rows, ny), link),
            pltpu.VMEM((nslab, depth, rows, ny), BF16),
            pltpu.VMEM((nz, rows, ny), BF16),
            pltpu.VMEM((nslab, depth + 2, rows, ny), BF16),
            pltpu.VMEM((nslab, depth + 2, rows, ny), BF16),
            pltpu.VMEM((ch * ny, depth * nx), BF16),
            pltpu.VMEM((ch // 2, 9 * ny, 2 * ny), BF16),
            pltpu.VMEM((27, ch, ny), F32),
            pltpu.VMEM((depth * nx, 9 * ny), BF16),
            pltpu.VMEM((ch // 2, 2 * TAP_ROWS, ny), F32),
            pltpu.VMEM((8, 128), F32),
            pltpu.VMEM((nslab, 8, 128), F32),
            pltpu.VMEM((8, 128), F32),
            pltpu.VMEM((nbox, 8, 128), F32),
            dma((8,)),
            dma,
            dma((nslab,)),
            dma((nslab,)),
            dma((nslab,)),
            dma((nslab,)),
            dma((nslab,)),
            dma((nslab,)),
            dma((nslab,)),
            dma((nslab,)),
            dma((nslab,)),
            dma((nslab,)),
            dma((nbox,)),
            dma((nbox,)),
        ],
        compiler_params=pltpu.CompilerParams(
            collective_id=0, has_side_effects=True, vmem_limit_bytes=int(44 * 2**20)
        ),
    )(
        *(
            pltpu.with_memory_space_constraint(x, pltpu.HBM)
            for x in (
                box_lower,
                box_upper,
                plane_lower,
                plane_upper,
                weight_lower,
                weight_upper,
                cone_grad,
                conv_weight,
                hidden_field.reshape(ch, depth, nx, ny),
            )
        )
    )
    return hidden_grad.reshape(hidden_field.shape), weight_grad


def solution(mesh):
    in_specs = (
        P("box", None, "slab", None, None),
        P(("box", "slab"), None, None),
        P(),
        P(("box", "slab")),
        P(("box", "slab")),
        P(("box", "slab")),
        P(("box", "slab")),
        P(("box", "slab")),
        P(("box", "slab")),
    )
    out_specs = (P("box", None, "slab", None, None), P())
    return jax.shard_map(
        functools.partial(local, mesh.shape["box"], mesh.shape["slab"]),
        mesh=mesh,
        in_specs=in_specs,
        out_specs=out_specs,
        check_vma=False,
    )
```

profile of v0, /device:TPU:0, one launch (start us, length us, event | category | flops | bytes accessed | tf_op | source)
XLA Modules:
  0.0 34.5 jit_solution(5029127071410872722)
XLA Ops:
  0.6 31.9 %shard_map.104 = (bf16[8,8,128,128]{3,2,1,0:T(8,128)(2,1)S(1)}, f32[8,27]{1,0:T(8,128)S(1)}) custom-call(s32[8]{0:T(128)} %bl_hbm.1, s32[8]{0:T(128)} %bu_hbm.1, s32[8]{0:T(128)} %plo_hbm.1, s32[8]{0:T(128)} %pup_hbm.1, s32[8]{0:T(128)} %wl_hbm.1, s32[8]{0:T(128)} %wu_hbm.1, f32[8,128,128]{2,1,0:T(8,128)} %cone_hbm.1, bf16[8,27]{1,0:T(8,128)(2,1)} %weight_hbm.1, ...), custom_call_target="tpu_custom_call" | custom-call | tf_op jit(solution)/shard_map/pallas_call | solution.py:410
  32.5 1.3 %copy.13 = bf16[1,8,8,128,128]{4,3,2,1,0:T(8,128)(2,1)} copy(bf16[1,8,8,128,128]{4,3,2,1,0:T(8,128)(2,1)S(1)} %bitcast.2) | data formatting | bytes 4194304
  33.9 0.6 %copy.14 = f32[8,27]{1,0:T(8,128)} copy(f32[8,27]{1,0:T(8,128)S(1)} %get-tuple-element.11) | data formatting | bytes 1728
where the time goes:
time: 34.6 us; the launch traced here: 34.5 us
  Pallas kernels  31.9 us (92%)
  local copies, waits for them, and re-layouts  1.91 us (6%)
  between operations  0.64 us (2%)
    pallas_call x1, Pallas kernels, local(): pl.pallas_call(functools.partial(kernel, nbox, nslab, scale), out_shape=(...  31.9 us
    unnamed x2, local copies, waits for them, and re-layouts  1.91 us

commit v1 on v0

v1 whole, which is shorter than its diff:
```python
import functools
import math

import jax
import jax.numpy as jnp
from jax import lax
from jax.experimental import pallas as pl
from jax.experimental.pallas import tpu as pltpu
from jax.sharding import PartitionSpec as P

WDEN = 256
MESH = pl.DeviceIdType.MESH
F32 = jnp.float32
BF16 = jnp.bfloat16
CHUNK = 32
EDGE = 8
NT = (((1,), (1,)), ((), ()))


def split(nx, nslab):
    rows = nx // nslab
    halves = 2 if rows % 16 == 0 else 1
    return halves, rows // halves


def kernel(nbox, nslab, scale, names, *refs):
    r = dict(zip(names, refs, strict=True))
    cone, weight, hbuf, out, wg = r["cone"], r["weight"], r["hbuf"], r["out"], r["wg"]
    bl, bu, plo, pup, wl, wu = (r[n] for n in ("bl", "bu", "plo", "pup", "wl", "wu"))
    own, z_up, z_dn = r["own"], r["z_up"], r["z_dn"]
    from_above, from_below = r["from_above"], r["from_below"]
    ht, wide, wmat, lmat, ft = r["ht"], r["wide"], r["wmat"], r["lmat"], r["ft"]
    msg, slab_terms, msg2, box_terms = r["msg"], r["slab_terms"], r["msg2"], r["box_terms"]

    g = lax.axis_index("box")
    me = lax.axis_index("slab")
    depth, nx, ny = cone.shape
    halves, rows = split(nx, nslab)
    part = nx // halves
    nz = depth * nslab
    ch = hbuf.shape[0]
    pairs = ch // 2
    chunks = ny // CHUNK
    window = CHUNK + 2 * EDGE
    send_a = [r["send_a%d" % h] for h in range(halves)]
    recv_a = [r["recv_a%d" % h] for h in range(halves)]
    send_b = [r["send_b%d" % h] for h in range(halves)]
    recv_b = [r["recv_b%d" % h] for h in range(halves)]

    smalls = [
        pltpu.make_async_copy(r[n + "_hbm"], r[n], r["isem"].at[i])
        for i, n in enumerate(("bl", "bu", "wl", "wu", "plo", "pup", "weight"))
    ]
    planes = [
        pltpu.make_async_copy(
            r["cone_hbm"].at[:, h * part : (h + 1) * part],
            cone.at[:, h * part : (h + 1) * part],
            r["csem"].at[h],
        )
        for h in range(halves)
    ]
    h_copy = pltpu.make_async_copy(r["h_hbm"], hbuf, r["hsem"].at[0])
    planes[0].start()
    for load in smalls:
        load.start()
    for load in planes[1:]:
        load.start()
    h_copy.start()

    barrier = pltpu.get_barrier_semaphore()

    def greet_slab(j, _):
        pl.semaphore_signal(barrier, inc=1, device_id={"slab": lax.rem(me + j, nslab)}, device_id_type=MESH)
        return 0

    def greet_box(j, _):
        pl.semaphore_signal(barrier, inc=1, device_id={"box": lax.rem(g + j, nbox)}, device_id_type=MESH)
        return 0

    lax.fori_loop(1, nslab, greet_slab, 0)
    lax.fori_loop(1, nbox, greet_box, 0)

    def weigh(h):
        def one(i, _):
            lower = wl[i].astype(F32) * (1.0 / WDEN)
            upper = wu[i].astype(F32) * (1.0 / WDEN)
            own_c = jnp.where(bl[i] == g, lower, 0.0) + jnp.where(bu[i] == g, upper, 0.0)
            below_c = jnp.where(bl[i] == g - 1, lower, 0.0)
            above_c = jnp.where(bu[i] == g + 1, upper, 0.0)
            plane = cone[i, h * part : (h + 1) * part].reshape(nslab, rows, ny)
            z_up[h, :, i] = (above_c * plane).astype(BF16)
            z_dn[h, :, i] = (below_c * plane).astype(BF16)
            own[h, :, i] = own_c * plane
            return 0

        lax.fori_loop(0, depth, one, 0)

    def up_copy(h, t):
        return pltpu.make_async_remote_copy(
            src_ref=z_up.at[h, t],
            dst_ref=from_below.at[h, t],
            send_sem=r["up_s"].at[h, t],
            recv_sem=r["up_r"].at[h, t],
            device_id={"box": lax.rem(g + 1, nbox)},
            device_id_type=MESH,
        )

    def dn_copy(h, t):
        return pltpu.make_async_remote_copy(
            src_ref=z_dn.at[h, t],
            dst_ref=from_above.at[h, t],
            send_sem=r["dn_s"].at[h, t],
            recv_sem=r["dn_r"].at[h, t],
            device_id={"box": lax.rem(g + nbox - 1, nbox)},
            device_id_type=MESH,
        )

    def send_z(h):
        def one(j, _):
            t = lax.rem(me + 1 + j, nslab)

            @pl.when(g < nbox - 1)
            def _():
                up_copy(h, t).start()

            @pl.when(g > 0)
            def _():
                dn_copy(h, t).start()

            return 0

        lax.fori_loop(0, nslab, one, 0)

    def a_copy(h, t, source):
        return pltpu.make_async_remote_copy(
            src_ref=send_a[h].at[t],
            dst_ref=recv_a[h].at[pl.ds(source * depth, depth)],
            send_sem=r["a_s"].at[h, t],
            recv_sem=r["a_r"].at[h, source],
            device_id={"slab": t},
            device_id_type=MESH,
        )

    def merge(h, t):
        @pl.when(g < nbox - 1)
        def _():
            dn_copy(h, t).wait_recv()
            own[h, t] = own[h, t] + from_above[h, t].astype(F32)

        @pl.when(g > 0)
        def _():
            up_copy(h, t).wait_recv()
            own[h, t] = own[h, t] + from_below[h, t].astype(F32)

    def merge_send(h, first, last, beside=None):
        def one(j, _):
            t = lax.rem(me + 1 + j, nslab)
            merge(h, t)
            send_a[h][t] = own[h, t].astype(BF16)
            a_copy(h, t, me).start()
            if beside is not None:
                beside(j)
            return 0

        lax.fori_loop(first, min(last, nslab - 1), one, 0)
        if last == nslab:
            merge(h, me)
            recv_a[h][pl.ds(me * depth, depth)] = own[h, me].astype(BF16)

    def wait_a(h):
        def one(j, _):
            source = lax.rem(me + j, nslab)
            a_copy(h, source, source).wait_recv()
            return 0

        lax.fori_loop(1, nslab, one, 0)

    def b_copy(h, s, source):
        return pltpu.make_async_remote_copy(
            src_ref=send_b[h].at[s],
            dst_ref=recv_b[h].at[source],
            send_sem=r["b_s"].at[h, s],
            recv_sem=r["b_r"].at[h, source],
            device_id={"slab": s},
            device_id_type=MESH,
        )

    def turn_send(h):
        offset = jnp.where(bl[0] == g, plo[0], pup[0]) - me * depth

        def wanted(s, q):
            return recv_a[h][lax.rem(s * depth - 1 + q - offset + 2 * nz, nz)]

        def one(j, _):
            s = lax.rem(me + 1 + j, nslab)
            for q in range(depth + 2):
                send_b[h][s, q] = wanted(s, q)
            b_copy(h, s, me).start()
            return 0

        lax.fori_loop(0, nslab - 1, one, 0)
        for q in range(depth + 2):
            recv_b[h][me, q] = wanted(me, q)

    def wait_b(h):
        def one(j, _):
            source = lax.rem(me + j, nslab)
            b_copy(h, source, source).wait_recv()
            return 0

        lax.fori_loop(1, nslab, one, 0)

    def turn(c):
        for z in range(depth):
            turned = hbuf[c, z].T
            for q in range(chunks):
                ht[q, pl.ds(pl.multiple_of(c * CHUNK, CHUNK), CHUNK), z * nx : (z + 1) * nx] = turned[
                    q * CHUNK : (q + 1) * CHUNK
                ]

    def turn_beside(j):
        @pl.when(j < ch)
        def _():
            turn(j)

    def fill_taps():
        y_in = lax.broadcasted_iota(jnp.int32, (ny, ny), 0)
        y_out = lax.broadcasted_iota(jnp.int32, (ny, ny), 1)
        hits = [y_in == lax.rem(y_out - dy + ny, ny) for dy in (-1, 0, 1)]
        taps = weight[...].astype(F32)
        for k in range(27):
            wide[k] = jnp.broadcast_to(taps[:, k : k + 1], (ch, ny))

        def one(p, _):
            for cc in range(2):
                for j in range(9):
                    block = jnp.zeros((ny, ny), F32)
                    for d in range(3):
                        block = jnp.where(hits[d], wide[3 * j + d, pl.ds(2 * p + cc, 1)], block)
                    wmat[p, j * ny : (j + 1) * ny, cc * ny : (cc + 1) * ny] = block.astype(BF16)
            return 0

        lax.fori_loop(0, pairs, one, 0)

    for load in smalls:
        load.wait()
    planes[0].wait()
    weigh(0)
    pl.semaphore_wait(barrier, nslab - 1 + nbox - 1)
    send_z(0)
    for h in range(1, halves):
        planes[h].wait()
        weigh(h)
        send_z(h)

    fill_taps()
    h_copy.wait()
    merge_send(0, 0, nslab, turn_beside)
    for c in range(nslab - 1, ch):
        turn(c)
    for h in range(1, halves):
        merge_send(h, 0, nslab // 2)
        wait_a(h - 1)
        turn_send(h - 1)
        merge_send(h, nslab // 2, nslab)
    wait_a(halves - 1)
    turn_send(halves - 1)
    for h in range(halves):
        wait_b(h)

    for q in range(depth + 2):
        plane = jnp.concatenate([recv_b[h][:, q].astype(F32).reshape(part, ny) for h in range(halves)], axis=0)
        for dx in (-1, 0, 1):
            moved = (plane if dx == 0 else pltpu.roll(plane, dx % nx, 0)).astype(BF16)
            for dz in (-1, 0, 1):
                z, j = q + dz - 1, (dz + 1) * 3 + dx + 1
                if 0 <= z < depth:
                    lmat[z * nx : (z + 1) * nx, j * ny : (j + 1) * ny] = moved
            turned = moved.T
            at = slice(q * nx, (q + 1) * nx)
            ft[dx + 1, EDGE : EDGE + ny, at] = turned
            ft[dx + 1, 0:EDGE, at] = turned[ny - EDGE : ny]
            ft[dx + 1, EDGE + ny : EDGE + ny + EDGE, at] = turned[0:EDGE]

    product = None
    for q in range(chunks):
        field = jnp.concatenate(
            [
                ft[dx + 1, q * CHUNK : q * CHUNK + window, (1 - dz) * nx : (1 - dz + depth) * nx]
                for dz in (-1, 0, 1)
                for dx in (-1, 0, 1)
            ],
            axis=0,
        )
        term = lax.dot_general(field, ht[q], NT, preferred_element_type=F32)
        product = term if product is None else product + term
    product = product.reshape(9, window, ch * CHUNK)
    w_row = lax.broadcasted_iota(jnp.int32, (window, ch * CHUNK), 0)
    w_y = lax.rem(lax.broadcasted_iota(jnp.int32, (window, ch * CHUNK), 1), CHUNK)
    picks = [w_row == w_y + EDGE - dy for dy in (-1, 0, 1)]
    sums = [
        jnp.sum(jnp.where(picks[d], product[j], 0.0), axis=0, keepdims=True) for j in range(9) for d in range(3)
    ]
    sums.append(jnp.zeros((5, ch * CHUNK), F32))
    by_tap = jnp.concatenate(sums, axis=0)
    msg[...] = jnp.zeros_like(msg)
    msg[:, 0:32] = jnp.sum(by_tap.T.reshape(ch, CHUNK, 32), axis=1)

    def c_copy(s, source):
        return pltpu.make_async_remote_copy(
            src_ref=msg,
            dst_ref=slab_terms.at[source],
            send_sem=r["c_s"].at[s],
            recv_sem=r["c_r"].at[source],
            device_id={"slab": s},
            device_id_type=MESH,
        )

    def d_copy(b, source):
        return pltpu.make_async_remote_copy(
            src_ref=msg2,
            dst_ref=box_terms.at[source],
            send_sem=r["d_s"].at[b],
            recv_sem=r["d_r"].at[source],
            device_id={"box": b},
            device_id_type=MESH,
        )

    def send_c(j, _):
        c_copy(lax.rem(me + j, nslab), me).start()
        return 0

    def send_d(j, _):
        d_copy(lax.rem(g + j, nbox), g).start()
        return 0

    def wait_c(j, _):
        source = lax.rem(me + j, nslab)
        c_copy(source, source).wait_recv()
        return 0

    def wait_d(j, _):
        source = lax.rem(g + j, nbox)
        d_copy(source, source).wait_recv()
        return 0

    def pair_grads(p, _):
        grads = jnp.dot(lmat[...], wmat[p], preferred_element_type=F32)
        for cc in range(2):
            out[2 * p + cc] = grads[:, cc * ny : (cc + 1) * ny].reshape(depth, nx, ny).astype(BF16)
        return 0

    slab_terms[me] = msg[...]
    lax.fori_loop(1, nslab, send_c, 0)
    lax.fori_loop(0, pairs // 2, pair_grads, 0)
    lax.fori_loop(1, nslab, wait_c, 0)
    total = slab_terms[0]
    for s in range(1, nslab):
        total = total + slab_terms[s]
    msg2[...] = total
    box_terms[g] = total
    lax.fori_loop(1, nbox, send_d, 0)
    lax.fori_loop(pairs // 2, pairs, pair_grads, 0)
    lax.fori_loop(1, nbox, wait_d, 0)
    total = box_terms[0]
    for b in range(1, nbox):
        total = total + box_terms[b]
    wg[...] = (total * scale)[:, 0:27]

    def drain_z(t, _):
        for h in range(halves):

            @pl.when(g < nbox - 1)
            def _():
                up_copy(h, t).wait_send()

            @pl.when(g > 0)
            def _():
                dn_copy(h, t).wait_send()

        return 0

    def drain_slab(j, _):
        s = lax.rem(me + j, nslab)
        for h in range(halves):
            a_copy(h, s, me).wait_send()
            b_copy(h, s, me).wait_send()
        c_copy(s, me).wait_send()
        return 0

    def drain_box(j, _):
        d_copy(lax.rem(g + j, nbox), g).wait_send()
        return 0

    lax.fori_loop(0, nslab, drain_z, 0)
    lax.fori_loop(1, nslab, drain_slab, 0)
    lax.fori_loop(1, nbox, drain_box, 0)


def local(
    nbox,
    nslab,
    hidden_field,
    cone_grad,
    conv_weight,
    box_lower,
    box_upper,
    plane_lower,
    plane_upper,
    weight_lower,
    weight_upper,
):
    _, ch, depth, nx, ny = hidden_field.shape
    halves, rows = split(nx, nslab)
    nz = depth * nslab
    scale = 1.0 / math.sqrt(nbox * nz * nx * ny)
    vmem = pl.BlockSpec(memory_space=pltpu.VMEM)
    hbm = pl.BlockSpec(memory_space=pltpu.HBM)
    dma = pltpu.SemaphoreType.DMA
    ins = {
        "bl_hbm": box_lower,
        "bu_hbm": box_upper,
        "plo_hbm": plane_lower,
        "pup_hbm": plane_upper,
        "wl_hbm": weight_lower,
        "wu_hbm": weight_upper,
        "cone_hbm": cone_grad,
        "weight_hbm": conv_weight,
        "h_hbm": hidden_field.reshape(ch, depth, nx, ny),
    }
    chunk = (halves, nslab, depth, rows, ny)
    scratch = {n: pltpu.SMEM((depth,), jnp.int32) for n in ("bl", "bu", "plo", "pup", "wl", "wu")}
    scratch["cone"] = pltpu.VMEM(cone_grad.shape, F32)
    scratch["weight"] = pltpu.VMEM(conv_weight.shape, BF16)
    scratch["hbuf"] = pltpu.VMEM((ch, depth, nx, ny), BF16)
    scratch["own"] = pltpu.VMEM(chunk, F32)
    for n in ("z_up", "z_dn", "from_above", "from_below"):
        scratch[n] = pltpu.VMEM(chunk, BF16)
    for h in range(halves):
        scratch["send_a%d" % h] = pltpu.VMEM(chunk[1:], BF16)
        scratch["recv_a%d" % h] = pltpu.VMEM((nz, rows, ny), BF16)
        scratch["send_b%d" % h] = pltpu.VMEM((nslab, depth + 2, rows, ny), BF16)
        scratch["recv_b%d" % h] = pltpu.VMEM((nslab, depth + 2, rows, ny), BF16)
    scratch["ht"] = pltpu.VMEM((ny // CHUNK, ch * CHUNK, depth * nx), BF16)
    scratch["wide"] = pltpu.VMEM((27, ch, ny), F32)
    scratch["wmat"] = pltpu.VMEM((ch // 2, 9 * ny, 2 * ny), BF16)
    scratch["lmat"] = pltpu.VMEM((depth * nx, 9 * ny), BF16)
    scratch["ft"] = pltpu.VMEM((3, ny + 2 * EDGE, (depth + 2) * nx), BF16)
    scratch["msg"] = pltpu.VMEM((ch, 128), F32)
    scratch["slab_terms"] = pltpu.VMEM((nslab, ch, 128), F32)
    scratch["msg2"] = pltpu.VMEM((ch, 128), F32)
    scratch["box_terms"] = pltpu.VMEM((nbox, ch, 128), F32)
    scratch["isem"] = dma((7,))
    scratch["csem"] = dma((halves,))
    scratch["hsem"] = dma((1,))
    for n in ("up", "dn", "a", "b"):
        scratch[n + "_s"] = dma((halves, nslab))
        scratch[n + "_r"] = dma((halves, nslab))
    scratch["c_s"] = dma((nslab,))
    scratch["c_r"] = dma((nslab,))
    scratch["d_s"] = dma((nbox,))
    scratch["d_r"] = dma((nbox,))
    names = (*ins, "out", "wg", *scratch)
    hidden_grad, weight_grad = pl.pallas_call(
        functools.partial(kernel, nbox, nslab, scale, names),
        out_shape=(
            pltpu.VMEM((ch, depth, nx, ny), BF16),
            jax.ShapeDtypeStruct((ch, 27), F32),
        ),
        in_specs=[hbm] * len(ins),
        out_specs=(vmem, vmem),
        scratch_shapes=list(scratch.values()),
        compiler_params=pltpu.CompilerParams(
            collective_id=0, has_side_effects=True, vmem_limit_bytes=int(44 * 2**20)
        ),
    )(*(pltpu.with_memory_space_constraint(x, pltpu.HBM) for x in ins.values()))
    return hidden_grad.reshape(hidden_field.shape), weight_grad


def solution(mesh):
    in_specs = (
        P("box", None, "slab", None, None),
        P(("box", "slab"), None, None),
        P(),
        P(("box", "slab")),
        P(("box", "slab")),
        P(("box", "slab")),
        P(("box", "slab")),
        P(("box", "slab")),
        P(("box", "slab")),
    )
    out_specs = (P("box", None, "slab", None, None), P())
    return jax.shard_map(
        functools.partial(local, mesh.shape["box"], mesh.shape["slab"]),
        mesh=mesh,
        in_specs=in_specs,
        out_specs=out_specs,
        check_vma=False,
    )
```

time: 34.6 us -> 33.4 us (0.965)
  Pallas kernels: 31.9 us -> 30.7 us
    pallas_call x1, Pallas kernels: 31.9 us -> 30.7 us  [local(): pl.pallas_call(functools.partial(kernel, nbox, nslab, scale, names), out_...]
where the time goes in v1:
time: 33.4 us; the launch traced here: 33.2 us
  Pallas kernels  30.7 us (92%)
  local copies, waits for them, and re-layouts  1.91 us (6%)
  between operations  0.64 us (2%)
    pallas_call x1, Pallas kernels, local(): pl.pallas_call(functools.partial(kernel, nbox, nslab, scale, names), out_...  30.7 us
    unnamed x2, local copies, waits for them, and re-layouts  1.91 us

profile of v1, /device:TPU:0, one launch (start us, length us, event | category | flops | bytes accessed | tf_op | source)
XLA Modules:
  0.0 33.2 jit_solution(8603052340295922493)
XLA Ops:
  0.6 30.7 %shard_map.104 = (bf16[8,8,128,128]{3,2,1,0:T(8,128)(2,1)S(1)}, f32[8,27]{1,0:T(8,128)S(1)}) custom-call(s32[8]{0:T(128)} %refs_0_.1, s32[8]{0:T(128)} %refs_1_.1, s32[8]{0:T(128)} %refs_2_.1, s32[8]{0:T(128)} %refs_3_.1, s32[8]{0:T(128)} %refs_4_.1, s32[8]{0:T(128)} %refs_5_.1, f32[8,128,128]{2,1,0:T(8,128)} %refs_6_.1, bf16[8,27]{1,0:T(8,128)(2,1)} %refs_7_.1, ...), custom_call_target="tpu_custom_call" | custom-call | tf_op jit(solution)/shard_map/pallas_call | solution.py:464
  31.3 1.3 %copy.13 = bf16[1,8,8,128,128]{4,3,2,1,0:T(8,128)(2,1)} copy(bf16[1,8,8,128,128]{4,3,2,1,0:T(8,128)(2,1)S(1)} %bitcast.2) | data formatting | bytes 4194304
  32.7 0.6 %copy.14 = f32[8,27]{1,0:T(8,128)} copy(f32[8,27]{1,0:T(8,128)S(1)} %get-tuple-element.11) | data formatting | bytes 1728

commit v2 on v1

--- a/solution.py
+++ b/solution.py
@@ -30,7 +30,7 @@
     own, z_up, z_dn = r["own"], r["z_up"], r["z_dn"]
     from_above, from_below = r["from_above"], r["from_below"]
     ht, wide, wmat, lmat, ft = r["ht"], r["wide"], r["wmat"], r["lmat"], r["ft"]
-    msg, slab_terms, msg2, box_terms = r["msg"], r["slab_terms"], r["msg2"], r["box_terms"]
+    msg, terms = r["msg"], r["terms"]
 
     g = lax.axis_index("box")
     me = lax.axis_index("slab")
@@ -152,7 +152,7 @@
             up_copy(h, t).wait_recv()
             own[h, t] = own[h, t] + from_below[h, t].astype(F32)
 
-    def merge_send(h, first, last, beside=None):
+    def merge_send(h, beside=None):
         def one(j, _):
             t = lax.rem(me + 1 + j, nslab)
             merge(h, t)
@@ -162,10 +162,9 @@
                 beside(j)
             return 0
 
-        lax.fori_loop(first, min(last, nslab - 1), one, 0)
-        if last == nslab:
-            merge(h, me)
-            recv_a[h][pl.ds(me * depth, depth)] = own[h, me].astype(BF16)
+        lax.fori_loop(0, nslab - 1, one, 0)
+        merge(h, me)
+        recv_a[h][pl.ds(me * depth, depth)] = own[h, me].astype(BF16)
 
     def wait_a(h):
         def one(j, _):
@@ -188,19 +187,22 @@
     def turn_send(h):
         offset = jnp.where(bl[0] == g, plo[0], pup[0]) - me * depth
 
-        def wanted(s, q):
-            return recv_a[h][lax.rem(s * depth - 1 + q - offset + 2 * nz, nz)]
+        def wanted(s):
+            first = lax.rem(s * depth - 1 - offset + 2 * nz, nz)
+            for q in range(depth + 2):
+                at = first + q
+                yield q, recv_a[h][jnp.where(at >= nz, at - nz, at)]
 
         def one(j, _):
             s = lax.rem(me + 1 + j, nslab)
-            for q in range(depth + 2):
-                send_b[h][s, q] = wanted(s, q)
+            for q, plane in wanted(s):
+                send_b[h][s, q] = plane
             b_copy(h, s, me).start()
             return 0
 
         lax.fori_loop(0, nslab - 1, one, 0)
-        for q in range(depth + 2):
-            recv_b[h][me, q] = wanted(me, q)
+        for q, plane in wanted(me):
+            recv_b[h][me, q] = plane
 
     def wait_b(h):
         def one(j, _):
@@ -255,14 +257,13 @@
 
     fill_taps()
     h_copy.wait()
-    merge_send(0, 0, nslab, turn_beside)
+    merge_send(0, turn_beside)
     for c in range(nslab - 1, ch):
         turn(c)
     for h in range(1, halves):
-        merge_send(h, 0, nslab // 2)
+        merge_send(h)
         wait_a(h - 1)
         turn_send(h - 1)
-        merge_send(h, nslab // 2, nslab)
     wait_a(halves - 1)
     turn_send(halves - 1)
     for h in range(halves):
@@ -303,45 +304,35 @@
     ]
     sums.append(jnp.zeros((5, ch * CHUNK), F32))
     by_tap = jnp.concatenate(sums, axis=0)
-    msg[...] = jnp.zeros_like(msg)
-    msg[:, 0:32] = jnp.sum(by_tap.T.reshape(ch, CHUNK, 32), axis=1)
-
-    def c_copy(s, source):
+    by_channel = jnp.sum(by_tap.T.reshape(ch, CHUNK, 32), axis=1)
+    by_channel = jnp.concatenate([by_channel, jnp.zeros((ch, 96), F32)], axis=1)
+    of_four = lax.rem(lax.broadcasted_iota(jnp.int32, (ch, 128), 0), 4)
+    packed = jnp.where(of_four == 0, by_channel, 0.0)
+    for i in range(1, 4):
+        packed = packed + pltpu.roll(jnp.where(of_four == i, by_channel, 0.0), 32 * i, 1)
+    packed = jnp.sum(packed.reshape(ch // 4, 4, 128), axis=1)
+    ndev = nbox * nslab
+    my = g * nslab + me
+    msg[...] = packed
+    terms[my] = packed
+
+    def r_copy(to, source):
         return pltpu.make_async_remote_copy(
             src_ref=msg,
-            dst_ref=slab_terms.at[source],
-            send_sem=r["c_s"].at[s],
-            recv_sem=r["c_r"].at[source],
-            device_id={"slab": s},
+            dst_ref=terms.at[source],
+            send_sem=r["r_s"].at[to],
+            recv_sem=r["r_r"].at[source],
+            device_id={"box": to // nslab, "slab": lax.rem(to, nslab)},
             device_id_type=MESH,
         )
 
-    def d_copy(b, source):
-        return pltpu.make_async_remote_copy(
-            src_ref=msg2,
-            dst_ref=box_terms.at[source],
-            send_sem=r["d_s"].at[b],
-            recv_sem=r["d_r"].at[source],
-            device_id={"box": b},
-            device_id_type=MESH,
-        )
-
-    def send_c(j, _):
-        c_copy(lax.rem(me + j, nslab), me).start()
-        return 0
-
-    def send_d(j, _):
-        d_copy(lax.rem(g + j, nbox), g).start()
-        return 0
-
-    def wait_c(j, _):
-        source = lax.rem(me + j, nslab)
-        c_copy(source, source).wait_recv()
-        return 0
-
-    def wait_d(j, _):
-        source = lax.rem(g + j, nbox)
-        d_copy(source, source).wait_recv()
+    def send_r(j, _):
+        r_copy(lax.rem(my + j, ndev), my).start()
+        return 0
+
+    def wait_r(j, _):
+        source = lax.rem(my + j, ndev)
+        r_copy(source, source).wait_recv()
         return 0
 
     def pair_grads(p, _):
@@ -350,22 +341,8 @@
             out[2 * p + cc] = grads[:, cc * ny : (cc + 1) * ny].reshape(depth, nx, ny).astype(BF16)
         return 0
 
-    slab_terms[me] = msg[...]
-    lax.fori_loop(1, nslab, send_c, 0)
-    lax.fori_loop(0, pairs // 2, pair_grads, 0)
-    lax.fori_loop(1, nslab, wait_c, 0)
-    total = slab_terms[0]
-    for s in range(1, nslab):
-        total = total + slab_terms[s]
-    msg2[...] = total
-    box_terms[g] = total
-    lax.fori_loop(1, nbox, send_d, 0)
-    lax.fori_loop(pairs // 2, pairs, pair_grads, 0)
-    lax.fori_loop(1, nbox, wait_d, 0)
-    total = box_terms[0]
-    for b in range(1, nbox):
-        total = total + box_terms[b]
-    wg[...] = (total * scale)[:, 0:27]
+    lax.fori_loop(1, ndev, send_r, 0)
+    lax.fori_loop(0, pairs, pair_grads, 0)
 
     def drain_z(t, _):
         for h in range(halves):
@@ -385,16 +362,28 @@
         for h in range(halves):
             a_copy(h, s, me).wait_send()
             b_copy(h, s, me).wait_send()
-        c_copy(s, me).wait_send()
-        return 0
-
-    def drain_box(j, _):
-        d_copy(lax.rem(g + j, nbox), g).wait_send()
+        return 0
+
+    def drain_r(j, _):
+        r_copy(lax.rem(my + j, ndev), my).wait_send()
         return 0
 
     lax.fori_loop(0, nslab, drain_z, 0)
     lax.fori_loop(1, nslab, drain_slab, 0)
-    lax.fori_loop(1, nbox, drain_box, 0)
+    lax.fori_loop(1, ndev, drain_r, 0)
+    lax.fori_loop(1, ndev, wait_r, 0)
+    total = jnp.sum(terms[...], axis=0) * scale
+    for c in range(ch):
+        wg[c : c + 1, :] = total[c // 4 : c // 4 + 1, (c % 4) * 32 : (c % 4) * 32 + 27]
+
+
+def write(grads, terms, out, wg, sem):
+    copies = [pltpu.make_async_copy(terms, wg, sem.at[0])]
+    copies += [pltpu.make_async_copy(grads.at[c], out.at[c], sem.at[c + 1]) for c in range(grads.shape[0])]
+    for copy in copies:
+        copy.start()
+    for copy in copies:
+        copy.wait()
 
 
 def local(
@@ -446,26 +435,22 @@
     scratch["wmat"] = pltpu.VMEM((ch // 2, 9 * ny, 2 * ny), BF16)
     scratch["lmat"] = pltpu.VMEM((depth * nx, 9 * ny), BF16)
     scratch["ft"] = pltpu.VMEM((3, ny + 2 * EDGE, (depth + 2) * nx), BF16)
-    scratch["msg"] = pltpu.VMEM((ch, 128), F32)
-    scratch["slab_terms"] = pltpu.VMEM((nslab, ch, 128), F32)
-    scratch["msg2"] = pltpu.VMEM((ch, 128), F32)
-    scratch["box_terms"] = pltpu.VMEM((nbox, ch, 128), F32)
+    scratch["msg"] = pltpu.VMEM((ch // 4, 128), F32)
+    scratch["terms"] = pltpu.VMEM((nbox * nslab, ch // 4, 128), F32)
     scratch["isem"] = dma((7,))
     scratch["csem"] = dma((halves,))
     scratch["hsem"] = dma((1,))
     for n in ("up", "dn", "a", "b"):
         scratch[n + "_s"] = dma((halves, nslab))
         scratch[n + "_r"] = dma((halves, nslab))
-    scratch["c_s"] = dma((nslab,))
-    scratch["c_r"] = dma((nslab,))
-    scratch["d_s"] = dma((nbox,))
-    scratch["d_r"] = dma((nbox,))
+    scratch["r_s"] = dma((nbox * nslab,))
+    scratch["r_r"] = dma((nbox * nslab,))
     names = (*ins, "out", "wg", *scratch)
     hidden_grad, weight_grad = pl.pallas_call(
         functools.partial(kernel, nbox, nslab, scale, names),
         out_shape=(
             pltpu.VMEM((ch, depth, nx, ny), BF16),
-            jax.ShapeDtypeStruct((ch, 27), F32),
+            pltpu.VMEM((ch, 27), F32),
         ),
         in_specs=[hbm] * len(ins),
         out_specs=(vmem, vmem),
@@ -474,6 +459,13 @@
             collective_id=0, has_side_effects=True, vmem_limit_bytes=int(44 * 2**20)
         ),
     )(*(pltpu.with_memory_space_constraint(x, pltpu.HBM) for x in ins.values()))
+    hidden_grad, weight_grad = pl.pallas_call(
+        write,
+        out_shape=(pltpu.HBM(hidden_grad.shape, BF16), pltpu.HBM(weight_grad.shape, F32)),
+        in_specs=[vmem, vmem],
+        out_specs=(hbm, hbm),
+        scratch_shapes=[dma((ch + 1,))],
+    )(pltpu.with_memory_space_constraint(hidden_grad, pltpu.VMEM), pltpu.with_memory_space_constraint(weight_grad, pltpu.VMEM))
     return hidden_grad.reshape(hidden_field.shape), weight_grad
 
 

time: 33.4 us -> 29.3 us (0.88)
  Pallas kernels: 30.7 us -> 28.5 us
  local copies, waits for them, and re-layouts: 1.91 us -> 0 us
    pallas_call x1, Pallas kernels: 30.7 us -> 27.1 us  [local(): pl.pallas_call(functools.partial(kernel, nbox, nslab, scale, names), out_...]
    unnamed x2 -> x0, local copies, waits for them, and re-layouts: 1.91 us -> none
    pallas_call x0 -> x1, Pallas kernels: none -> 1.39 us  [local(): pl.pallas_call(write, out_shape=(pltpu.HBM(hidden_grad.shape, BF16), pltp...]
where the time goes in v2:
time: 29.3 us; the launch traced here: 29.1 us
  Pallas kernels  28.5 us (97%)
  between operations  0.64 us (2%)
    pallas_call x1, Pallas kernels, local(): pl.pallas_call(functools.partial(kernel, nbox, nslab, scale, names), out_...  27.1 us
    pallas_call x1, Pallas kernels, local(): pl.pallas_call(write, out_shape=(pltpu.HBM(hidden_grad.shape, BF16), pltp...  1.39 us

profile of v2, /device:TPU:0, one launch (start us, length us, event | category | flops | bytes accessed | tf_op | source)
XLA Modules:
  0.0 29.1 jit_solution(7261338508547733708)
XLA Ops:
  0.6 27.1 %shard_map.104 = (bf16[8,8,128,128]{3,2,1,0:T(8,128)(2,1)S(1)}, f32[8,27]{1,0:T(8,128)S(1)}) custom-call(s32[8]{0:T(128)} %refs_0_.1, s32[8]{0:T(128)} %refs_1_.1, s32[8]{0:T(128)} %refs_2_.1, s32[8]{0:T(128)} %refs_3_.1, s32[8]{0:T(128)} %refs_4_.1, s32[8]{0:T(128)} %refs_5_.1, f32[8,128,128]{2,1,0:T(8,128)} %refs_6_.1, bf16[8,27]{1,0:T(8,128)(2,1)} %refs_7_.1, ...), custom_call_target="tpu_custom_call" | custom-call | tf_op jit(solution)/shard_map/pallas_call | solution.py:449
  27.7 1.4 %shard_map.105 = (bf16[8,8,128,128]{3,2,1,0:T(8,128)(2,1)}, f32[8,27]{1,0:T(8,128)}) custom-call(bf16[8,8,128,128]{3,2,1,0:T(8,128)(2,1)S(1)} %get-tuple-element.6.grads, f32[8,27]{1,0:T(8,128)S(1)} %get-tuple-element.7.terms), custom_call_target="tpu_custom_call" | custom-call | tf_op jit(solution)/shard_map/pallas_call | solution.py:462

commit v3 on v2

--- a/solution.py
+++ b/solution.py
@@ -21,6 +21,15 @@
     rows = nx // nslab
     halves = 2 if rows % 16 == 0 else 1
     return halves, rows // halves
+
+
+def other(at, j, size):
+    bit, partner = 1, at
+    while bit < size:
+        if j & bit:
+            partner = partner + bit * (1 - 2 * lax.rem(lax.div(at, bit), 2))
+        bit *= 2
+    return partner
 
 
 def kernel(nbox, nslab, scale, names, *refs):
@@ -95,11 +104,21 @@
 
         lax.fori_loop(0, depth, one, 0)
 
+    def every(source, target, send, recv, at):
+        return pltpu.make_async_remote_copy(
+            src_ref=source,
+            dst_ref=target,
+            send_sem=send.at[at],
+            recv_sem=recv.at[at],
+            device_id={"slab": me},
+            device_id_type=MESH,
+        )
+
     def up_copy(h, t):
         return pltpu.make_async_remote_copy(
             src_ref=z_up.at[h, t],
             dst_ref=from_below.at[h, t],
-            send_sem=r["up_s"].at[h, t],
+            send_sem=r["up_s"].at[0],
             recv_sem=r["up_r"].at[h, t],
             device_id={"box": lax.rem(g + 1, nbox)},
             device_id_type=MESH,
@@ -109,15 +128,15 @@
         return pltpu.make_async_remote_copy(
             src_ref=z_dn.at[h, t],
             dst_ref=from_above.at[h, t],
-            send_sem=r["dn_s"].at[h, t],
+            send_sem=r["dn_s"].at[0],
             recv_sem=r["dn_r"].at[h, t],
             device_id={"box": lax.rem(g + nbox - 1, nbox)},
             device_id_type=MESH,
         )
 
     def send_z(h):
-        def one(j, _):
-            t = lax.rem(me + 1 + j, nslab)
+        for j in reversed(range(nslab)):
+            t = other(me, j, nslab)
 
             @pl.when(g < nbox - 1)
             def _():
@@ -127,16 +146,12 @@
             def _():
                 dn_copy(h, t).start()
 
-            return 0
-
-        lax.fori_loop(0, nslab, one, 0)
-
     def a_copy(h, t, source):
         return pltpu.make_async_remote_copy(
             src_ref=send_a[h].at[t],
             dst_ref=recv_a[h].at[pl.ds(source * depth, depth)],
-            send_sem=r["a_s"].at[h, t],
-            recv_sem=r["a_r"].at[h, source],
+            send_sem=r["a_s"].at[h],
+            recv_sem=r["a_r"].at[h],
             device_id={"slab": t},
             device_id_type=MESH,
         )
@@ -153,33 +168,25 @@
             own[h, t] = own[h, t] + from_below[h, t].astype(F32)
 
     def merge_send(h, beside=None):
-        def one(j, _):
-            t = lax.rem(me + 1 + j, nslab)
+        for j in reversed(range(1, nslab)):
+            t = other(me, j, nslab)
             merge(h, t)
             send_a[h][t] = own[h, t].astype(BF16)
             a_copy(h, t, me).start()
             if beside is not None:
-                beside(j)
-            return 0
-
-        lax.fori_loop(0, nslab - 1, one, 0)
+                beside(nslab - 1 - j)
         merge(h, me)
         recv_a[h][pl.ds(me * depth, depth)] = own[h, me].astype(BF16)
 
     def wait_a(h):
-        def one(j, _):
-            source = lax.rem(me + j, nslab)
-            a_copy(h, source, source).wait_recv()
-            return 0
-
-        lax.fori_loop(1, nslab, one, 0)
+        every(send_a[h].at[: nslab - 1], recv_a[h].at[: (nslab - 1) * depth], r["a_s"], r["a_r"], h).wait_recv()
 
     def b_copy(h, s, source):
         return pltpu.make_async_remote_copy(
             src_ref=send_b[h].at[s],
             dst_ref=recv_b[h].at[source],
-            send_sem=r["b_s"].at[h, s],
-            recv_sem=r["b_r"].at[h, source],
+            send_sem=r["b_s"].at[h],
+            recv_sem=r["b_r"].at[h],
             device_id={"slab": s},
             device_id_type=MESH,
         )
@@ -193,24 +200,17 @@
                 at = first + q
                 yield q, recv_a[h][jnp.where(at >= nz, at - nz, at)]
 
-        def one(j, _):
-            s = lax.rem(me + 1 + j, nslab)
+        for j in reversed(range(1, nslab)):
+            s = other(me, j, nslab)
             for q, plane in wanted(s):
                 send_b[h][s, q] = plane
             b_copy(h, s, me).start()
-            return 0
-
-        lax.fori_loop(0, nslab - 1, one, 0)
+
         for q, plane in wanted(me):
             recv_b[h][me, q] = plane
 
     def wait_b(h):
-        def one(j, _):
-            source = lax.rem(me + j, nslab)
-            b_copy(h, source, source).wait_recv()
-            return 0
-
-        lax.fori_loop(1, nslab, one, 0)
+        every(send_b[h].at[: nslab - 1], recv_b[h].at[: nslab - 1], r["b_s"], r["b_r"], h).wait_recv()
 
     def turn(c):
         for z in range(depth):
@@ -221,8 +221,7 @@
                 ]
 
     def turn_beside(j):
-        @pl.when(j < ch)
-        def _():
+        if j < ch:
             turn(j)
 
     def fill_taps():
@@ -316,24 +315,19 @@
     msg[...] = packed
     terms[my] = packed
 
-    def r_copy(to, source):
+    def r_copy(b, s, source):
         return pltpu.make_async_remote_copy(
             src_ref=msg,
             dst_ref=terms.at[source],
-            send_sem=r["r_s"].at[to],
-            recv_sem=r["r_r"].at[source],
-            device_id={"box": to // nslab, "slab": lax.rem(to, nslab)},
-            device_id_type=MESH,
-        )
-
-    def send_r(j, _):
-        r_copy(lax.rem(my + j, ndev), my).start()
-        return 0
-
-    def wait_r(j, _):
-        source = lax.rem(my + j, ndev)
-        r_copy(source, source).wait_recv()
-        return 0
+            send_sem=r["r_s"].at[0],
+            recv_sem=r["r_r"].at[0],
+            device_id={"box": b, "slab": s},
+            device_id_type=MESH,
+        )
+
+    def send_r():
+        for j in reversed(range(1, ndev)):
+            r_copy(other(g, j // nslab, nbox), other(me, j % nslab, nslab), my).start()
 
     def pair_grads(p, _):
         grads = jnp.dot(lmat[...], wmat[p], preferred_element_type=F32)
@@ -341,37 +335,23 @@
             out[2 * p + cc] = grads[:, cc * ny : (cc + 1) * ny].reshape(depth, nx, ny).astype(BF16)
         return 0
 
-    lax.fori_loop(1, ndev, send_r, 0)
+    send_r()
     lax.fori_loop(0, pairs, pair_grads, 0)
 
-    def drain_z(t, _):
-        for h in range(halves):
-
-            @pl.when(g < nbox - 1)
-            def _():
-                up_copy(h, t).wait_send()
-
-            @pl.when(g > 0)
-            def _():
-                dn_copy(h, t).wait_send()
-
-        return 0
-
-    def drain_slab(j, _):
-        s = lax.rem(me + j, nslab)
-        for h in range(halves):
-            a_copy(h, s, me).wait_send()
-            b_copy(h, s, me).wait_send()
-        return 0
-
-    def drain_r(j, _):
-        r_copy(lax.rem(my + j, ndev), my).wait_send()
-        return 0
-
-    lax.fori_loop(0, nslab, drain_z, 0)
-    lax.fori_loop(1, nslab, drain_slab, 0)
-    lax.fori_loop(1, ndev, drain_r, 0)
-    lax.fori_loop(1, ndev, wait_r, 0)
+    @pl.when(g < nbox - 1)
+    def _():
+        every(z_up, from_below, r["up_s"], r["up_s"], 0).wait_send()
+
+    @pl.when(g > 0)
+    def _():
+        every(z_dn, from_above, r["dn_s"], r["dn_s"], 0).wait_send()
+
+    for h in range(halves):
+        every(send_a[h].at[: nslab - 1], recv_a[h].at[: (nslab - 1) * depth], r["a_s"], r["a_r"], h).wait_send()
+        every(send_b[h].at[: nslab - 1], recv_b[h].at[: nslab - 1], r["b_s"], r["b_r"], h).wait_send()
+    r_all = every(terms.at[: ndev - 1], terms.at[: ndev - 1], r["r_s"], r["r_r"], 0)
+    r_all.wait_send()
+    r_all.wait_recv()
     total = jnp.sum(terms[...], axis=0) * scale
     for c in range(ch):
         wg[c : c + 1, :] = total[c // 4 : c // 4 + 1, (c % 4) * 32 : (c % 4) * 32 + 27]
@@ -440,11 +420,14 @@
     scratch["isem"] = dma((7,))
     scratch["csem"] = dma((halves,))
     scratch["hsem"] = dma((1,))
-    for n in ("up", "dn", "a", "b"):
-        scratch[n + "_s"] = dma((halves, nslab))
+    for n in ("up", "dn"):
+        scratch[n + "_s"] = dma((1,))
         scratch[n + "_r"] = dma((halves, nslab))
-    scratch["r_s"] = dma((nbox * nslab,))
-    scratch["r_r"] = dma((nbox * nslab,))
+    for n in ("a", "b"):
+        scratch[n + "_s"] = dma((halves,))
+        scratch[n + "_r"] = dma((halves,))
+    scratch["r_s"] = dma((1,))
+    scratch["r_r"] = dma((1,))
     names = (*ins, "out", "wg", *scratch)
     hidden_grad, weight_grad = pl.pallas_call(
         functools.partial(kernel, nbox, nslab, scale, names),

time: 29.3 us -> 27.7 us (0.945)
  Pallas kernels: 28.5 us -> 26.9 us
    pallas_call x1, Pallas kernels: 27.1 us -> 25.5 us  [local(): pl.pallas_call(functools.partial(kernel, nbox, nslab, scale, names), out_...]
where the time goes in v3:
time: 27.7 us; the launch traced here: 27.5 us
  Pallas kernels  26.9 us (97%)
  between operations  0.64 us (2%)
    pallas_call x1, Pallas kernels, local(): pl.pallas_call(functools.partial(kernel, nbox, nslab, scale, names), out_...  25.5 us
    pallas_call x1, Pallas kernels, local(): pl.pallas_call(write, out_shape=(pltpu.HBM(hidden_grad.shape, BF16), pltp...  1.39 us

profile of v3, /device:TPU:0, one launch (start us, length us, event | category | flops | bytes accessed | tf_op | source)
XLA Modules:
  0.0 27.5 jit_solution(12731392678145266680)
XLA Ops:
  0.6 25.5 %shard_map.104 = (bf16[8,8,128,128]{3,2,1,0:T(8,128)(2,1)S(1)}, f32[8,27]{1,0:T(8,128)S(1)}) custom-call(s32[8]{0:T(128)} %refs_0_.1, s32[8]{0:T(128)} %refs_1_.1, s32[8]{0:T(128)} %refs_2_.1, s32[8]{0:T(128)} %refs_3_.1, s32[8]{0:T(128)} %refs_4_.1, s32[8]{0:T(128)} %refs_5_.1, f32[8,128,128]{2,1,0:T(8,128)} %refs_6_.1, bf16[8,27]{1,0:T(8,128)(2,1)} %refs_7_.1, ...), custom_call_target="tpu_custom_call" | custom-call | tf_op jit(solution)/shard_map/pallas_call | solution.py:432
  26.1 1.4 %shard_map.105 = (bf16[8,8,128,128]{3,2,1,0:T(8,128)(2,1)}, f32[8,27]{1,0:T(8,128)}) custom-call(bf16[8,8,128,128]{3,2,1,0:T(8,128)(2,1)S(1)} %get-tuple-element.6.grads, f32[8,27]{1,0:T(8,128)S(1)} %get-tuple-element.7.terms), custom_call_target="tpu_custom_call" | custom-call | tf_op jit(solution)/shard_map/pallas_call | solution.py:445

commit v4 on v3

--- a/solution.py
+++ b/solution.py
@@ -90,19 +90,19 @@
     lax.fori_loop(1, nbox, greet_box, 0)
 
     def weigh(h):
-        def one(i, _):
-            lower = wl[i].astype(F32) * (1.0 / WDEN)
-            upper = wu[i].astype(F32) * (1.0 / WDEN)
-            own_c = jnp.where(bl[i] == g, lower, 0.0) + jnp.where(bu[i] == g, upper, 0.0)
-            below_c = jnp.where(bl[i] == g - 1, lower, 0.0)
-            above_c = jnp.where(bu[i] == g + 1, upper, 0.0)
+        for i in range(depth):
+            below_c = jnp.where(bl[i] == g - 1, wl[i].astype(F32) * (1.0 / WDEN), 0.0)
+            above_c = jnp.where(bu[i] == g + 1, wu[i].astype(F32) * (1.0 / WDEN), 0.0)
             plane = cone[i, h * part : (h + 1) * part].reshape(nslab, rows, ny)
             z_up[h, :, i] = (above_c * plane).astype(BF16)
             z_dn[h, :, i] = (below_c * plane).astype(BF16)
-            own[h, :, i] = own_c * plane
-            return 0
-
-        lax.fori_loop(0, depth, one, 0)
+
+    def weigh_own(i, _):
+        lower = wl[i].astype(F32) * (1.0 / WDEN)
+        upper = wu[i].astype(F32) * (1.0 / WDEN)
+        own_c = jnp.where(bl[i] == g, lower, 0.0) + jnp.where(bu[i] == g, upper, 0.0)
+        own[:, :, i] = own_c * cone[i].reshape(halves, nslab, rows, ny)
+        return 0
 
     def every(source, target, send, recv, at):
         return pltpu.make_async_remote_copy(
@@ -114,37 +114,38 @@
             device_id_type=MESH,
         )
 
-    def up_copy(h, t):
-        return pltpu.make_async_remote_copy(
-            src_ref=z_up.at[h, t],
-            dst_ref=from_below.at[h, t],
+    def up_copy(h, c):
+        return pltpu.make_async_remote_copy(
+            src_ref=z_up.at[h, pl.ds(2 * c, 2)],
+            dst_ref=from_below.at[h, pl.ds(2 * c, 2)],
             send_sem=r["up_s"].at[0],
-            recv_sem=r["up_r"].at[h, t],
+            recv_sem=r["up_r"].at[h, c],
             device_id={"box": lax.rem(g + 1, nbox)},
             device_id_type=MESH,
         )
 
-    def dn_copy(h, t):
-        return pltpu.make_async_remote_copy(
-            src_ref=z_dn.at[h, t],
-            dst_ref=from_above.at[h, t],
+    def dn_copy(h, c):
+        return pltpu.make_async_remote_copy(
+            src_ref=z_dn.at[h, pl.ds(2 * c, 2)],
+            dst_ref=from_above.at[h, pl.ds(2 * c, 2)],
             send_sem=r["dn_s"].at[0],
-            recv_sem=r["dn_r"].at[h, t],
+            recv_sem=r["dn_r"].at[h, c],
             device_id={"box": lax.rem(g + nbox - 1, nbox)},
             device_id_type=MESH,
         )
 
-    def send_z(h):
-        for j in reversed(range(nslab)):
-            t = other(me, j, nslab)
+    chips = [other(lax.div(me, 2), j, nslab // 2) for j in reversed(range(nslab // 2))]
+
+    def send_z(h, which):
+        for c in which:
 
             @pl.when(g < nbox - 1)
             def _():
-                up_copy(h, t).start()
+                up_copy(h, c).start()
 
             @pl.when(g > 0)
             def _():
-                dn_copy(h, t).start()
+                dn_copy(h, c).start()
 
     def a_copy(h, t, source):
         return pltpu.make_async_remote_copy(
@@ -156,27 +157,30 @@
             device_id_type=MESH,
         )
 
-    def merge(h, t):
-        @pl.when(g < nbox - 1)
-        def _():
-            dn_copy(h, t).wait_recv()
-            own[h, t] = own[h, t] + from_above[h, t].astype(F32)
-
-        @pl.when(g > 0)
-        def _():
-            up_copy(h, t).wait_recv()
-            own[h, t] = own[h, t] + from_below[h, t].astype(F32)
-
-    def merge_send(h, beside=None):
-        for j in reversed(range(1, nslab)):
-            t = other(me, j, nslab)
-            merge(h, t)
-            send_a[h][t] = own[h, t].astype(BF16)
-            a_copy(h, t, me).start()
+    def merge_send(h, which, beside=None):
+        sibling = other(me, 1, nslab)
+        for n, c in which:
+
+            @pl.when(g < nbox - 1)
+            def _():
+                dn_copy(h, c).wait_recv()
+
+            @pl.when(g > 0)
+            def _():
+                up_copy(h, c).wait_recv()
+
+            def merged(t):
+                return (own[h, t] + from_above[h, t].astype(F32) + from_below[h, t].astype(F32)).astype(BF16)
+
+            last = n == len(chips) - 1
+            for t in (sibling, me) if last else (2 * c, 2 * c + 1):
+                if last and t is me:
+                    recv_a[h][pl.ds(me * depth, depth)] = merged(me)
+                else:
+                    send_a[h][t] = merged(t)
+                    a_copy(h, t, me).start()
             if beside is not None:
-                beside(nslab - 1 - j)
-        merge(h, me)
-        recv_a[h][pl.ds(me * depth, depth)] = own[h, me].astype(BF16)
+                beside(n)
 
     def wait_a(h):
         every(send_a[h].at[: nslab - 1], recv_a[h].at[: (nslab - 1) * depth], r["a_s"], r["a_r"], h).wait_recv()
@@ -194,20 +198,16 @@
     def turn_send(h):
         offset = jnp.where(bl[0] == g, plo[0], pup[0]) - me * depth
 
+        recv_a[h][nz:] = recv_a[h][: depth + 2]
+
         def wanted(s):
-            first = lax.rem(s * depth - 1 - offset + 2 * nz, nz)
-            for q in range(depth + 2):
-                at = first + q
-                yield q, recv_a[h][jnp.where(at >= nz, at - nz, at)]
+            return recv_a[h][pl.ds(lax.rem(s * depth - 1 - offset + 2 * nz, nz), depth + 2)]
 
         for j in reversed(range(1, nslab)):
             s = other(me, j, nslab)
-            for q, plane in wanted(s):
-                send_b[h][s, q] = plane
+            send_b[h][s] = wanted(s)
             b_copy(h, s, me).start()
-
-        for q, plane in wanted(me):
-            recv_b[h][me, q] = plane
+        recv_b[h][me] = wanted(me)
 
     def wait_b(h):
         every(send_b[h].at[: nslab - 1], recv_b[h].at[: nslab - 1], r["b_s"], r["b_r"], h).wait_recv()
@@ -220,9 +220,9 @@
                     q * CHUNK : (q + 1) * CHUNK
                 ]
 
-    def turn_beside(j):
-        if j < ch:
-            turn(j)
+    def turn_beside(n):
+        for c in range(n * ch // len(chips), (n + 1) * ch // len(chips)):
+            turn(c)
 
     def fill_taps():
         y_in = lax.broadcasted_iota(jnp.int32, (ny, ny), 0)
@@ -248,35 +248,48 @@
     planes[0].wait()
     weigh(0)
     pl.semaphore_wait(barrier, nslab - 1 + nbox - 1)
-    send_z(0)
+    send_z(0, chips[:-1])
     for h in range(1, halves):
         planes[h].wait()
         weigh(h)
-        send_z(h)
+        send_z(h, chips[:-1])
+    for h in range(halves):
+        send_z(h, chips[-1:])
+
+    lax.fori_loop(0, depth, weigh_own, 0)
+
+    @pl.when(g == nbox - 1)
+    def _():
+        from_above[...] = jnp.zeros_like(from_above)
+
+    @pl.when(g == 0)
+    def _():
+        from_below[...] = jnp.zeros_like(from_below)
 
     fill_taps()
     h_copy.wait()
-    merge_send(0, turn_beside)
-    for c in range(nslab - 1, ch):
-        turn(c)
+    order = list(enumerate(chips))
+    merge_send(0, order[:-1], turn_beside)
+    turn_beside(len(chips) - 1)
     for h in range(1, halves):
-        merge_send(h)
-        wait_a(h - 1)
-        turn_send(h - 1)
+        merge_send(h, order[:-1])
+    for h in range(halves):
+        merge_send(h, order[-1:])
+    for h in range(halves - 1):
+        wait_a(h)
+        turn_send(h)
     wait_a(halves - 1)
     turn_send(halves - 1)
     for h in range(halves):
         wait_b(h)
 
+    def moved(q, dx):
+        plane = jnp.concatenate([recv_b[h][:, q].astype(F32).reshape(part, ny) for h in range(halves)], axis=0)
+        return (plane if dx == 0 else pltpu.roll(plane, dx % nx, 0)).astype(BF16)
+
     for q in range(depth + 2):
-        plane = jnp.concatenate([recv_b[h][:, q].astype(F32).reshape(part, ny) for h in range(halves)], axis=0)
         for dx in (-1, 0, 1):
-            moved = (plane if dx == 0 else pltpu.roll(plane, dx % nx, 0)).astype(BF16)
-            for dz in (-1, 0, 1):
-                z, j = q + dz - 1, (dz + 1) * 3 + dx + 1
-                if 0 <= z < depth:
-                    lmat[z * nx : (z + 1) * nx, j * ny : (j + 1) * ny] = moved
-            turned = moved.T
+            turned = moved(q, dx).T
             at = slice(q * nx, (q + 1) * nx)
             ft[dx + 1, EDGE : EDGE + ny, at] = turned
             ft[dx + 1, 0:EDGE, at] = turned[ny - EDGE : ny]
@@ -336,6 +349,13 @@
         return 0
 
     send_r()
+    for q in range(depth + 2):
+        for dx in (-1, 0, 1):
+            plane = moved(q, dx)
+            for dz in (-1, 0, 1):
+                z, j = q + dz - 1, (dz + 1) * 3 + dx + 1
+                if 0 <= z < depth:
+                    lmat[z * nx : (z + 1) * nx, j * ny : (j + 1) * ny] = plane
     lax.fori_loop(0, pairs, pair_grads, 0)
 
     @pl.when(g < nbox - 1)
@@ -407,7 +427,7 @@
         scratch[n] = pltpu.VMEM(chunk, BF16)
     for h in range(halves):
         scratch["send_a%d" % h] = pltpu.VMEM(chunk[1:], BF16)
-        scratch["recv_a%d" % h] = pltpu.VMEM((nz, rows, ny), BF16)
+        scratch["recv_a%d" % h] = pltpu.VMEM((nz + depth + 2, rows, ny), BF16)
         scratch["send_b%d" % h] = pltpu.VMEM((nslab, depth + 2, rows, ny), BF16)
         scratch["recv_b%d" % h] = pltpu.VMEM((nslab, depth + 2, rows, ny), BF16)
     scratch["ht"] = pltpu.VMEM((ny // CHUNK, ch * CHUNK, depth * nx), BF16)
@@ -422,7 +442,7 @@
     scratch["hsem"] = dma((1,))
     for n in ("up", "dn"):
         scratch[n + "_s"] = dma((1,))
-        scratch[n + "_r"] = dma((halves, nslab))
+        scratch[n + "_r"] = dma((halves, nslab // 2))
     for n in ("a", "b"):
         scratch[n + "_s"] = dma((halves,))
         scratch[n + "_r"] = dma((halves,))

time: 27.7 us -> 27.1 us (0.978)
  Pallas kernels: 26.9 us -> 26.3 us
    pallas_call x1, Pallas kernels: 25.5 us -> 25 us  [local(): pl.pallas_call(functools.partial(kernel, nbox, nslab, scale, names), out_...]
where the time goes in v4:
time: 27.1 us; the launch traced here: 27 us
  Pallas kernels  26.3 us (97%)
  between operations  0.64 us (2%)
    pallas_call x1, Pallas kernels, local(): pl.pallas_call(functools.partial(kernel, nbox, nslab, scale, names), out_...  25 us
    pallas_call x1, Pallas kernels, local(): pl.pallas_call(write, out_shape=(pltpu.HBM(hidden_grad.shape, BF16), pltp...  1.39 us

profile of v4, /device:TPU:0, one launch (start us, length us, event | category | flops | bytes accessed | tf_op | source)
XLA Modules:
  0.0 27.0 jit_solution(15224321051618554988)
XLA Ops:
  0.6 25.0 %shard_map.104 = (bf16[8,8,128,128]{3,2,1,0:T(8,128)(2,1)S(1)}, f32[8,27]{1,0:T(8,128)S(1)}) custom-call(s32[8]{0:T(128)} %refs_0_.1, s32[8]{0:T(128)} %refs_1_.1, s32[8]{0:T(128)} %refs_2_.1, s32[8]{0:T(128)} %refs_3_.1, s32[8]{0:T(128)} %refs_4_.1, s32[8]{0:T(128)} %refs_5_.1, f32[8,128,128]{2,1,0:T(8,128)} %refs_6_.1, bf16[8,27]{1,0:T(8,128)(2,1)} %refs_7_.1, ...), custom_call_target="tpu_custom_call" | custom-call | tf_op jit(solution)/shard_map/pallas_call | solution.py:452
  25.6 1.4 %shard_map.105 = (bf16[8,8,128,128]{3,2,1,0:T(8,128)(2,1)}, f32[8,27]{1,0:T(8,128)}) custom-call(bf16[8,8,128,128]{3,2,1,0:T(8,128)(2,1)S(1)} %get-tuple-element.6.grads, f32[8,27]{1,0:T(8,128)S(1)} %get-tuple-element.7.terms), custom_call_target="tpu_custom_call" | custom-call | tf_op jit(solution)/shard_map/pallas_call | solution.py:465

commit v5 on v4

--- a/solution.py
+++ b/solution.py
@@ -14,7 +14,6 @@
 BF16 = jnp.bfloat16
 CHUNK = 32
 EDGE = 8
-NT = (((1,), (1,)), ((), ()))
 
 
 def split(nx, nslab):
@@ -38,7 +37,7 @@
     bl, bu, plo, pup, wl, wu = (r[n] for n in ("bl", "bu", "plo", "pup", "wl", "wu"))
     own, z_up, z_dn = r["own"], r["z_up"], r["z_dn"]
     from_above, from_below = r["from_above"], r["from_below"]
-    ht, wide, wmat, lmat, ft = r["ht"], r["wide"], r["wmat"], r["lmat"], r["ft"]
+    shifted, wide, wmat, lmat, product = r["shifted"], r["wide"], r["wmat"], r["lmat"], r["product"]
     msg, terms = r["msg"], r["terms"]
 
     g = lax.axis_index("box")
@@ -51,6 +50,7 @@
     pairs = ch // 2
     chunks = ny // CHUNK
     window = CHUNK + 2 * EDGE
+    wide_n = ch * CHUNK
     send_a = [r["send_a%d" % h] for h in range(halves)]
     recv_a = [r["recv_a%d" % h] for h in range(halves)]
     send_b = [r["send_b%d" % h] for h in range(halves)]
@@ -157,7 +157,7 @@
             device_id_type=MESH,
         )
 
-    def merge_send(h, which, beside=None):
+    def merge_send(h, which):
         sibling = other(me, 1, nslab)
         for n, c in which:
 
@@ -179,9 +179,6 @@
                 else:
                     send_a[h][t] = merged(t)
                     a_copy(h, t, me).start()
-            if beside is not None:
-                beside(n)
-
     def wait_a(h):
         every(send_a[h].at[: nslab - 1], recv_a[h].at[: (nslab - 1) * depth], r["a_s"], r["a_r"], h).wait_recv()
 
@@ -212,17 +209,45 @@
     def wait_b(h):
         every(send_b[h].at[: nslab - 1], recv_b[h].at[: nslab - 1], r["b_s"], r["b_r"], h).wait_recv()
 
-    def turn(c):
-        for z in range(depth):
-            turned = hbuf[c, z].T
-            for q in range(chunks):
-                ht[q, pl.ds(pl.multiple_of(c * CHUNK, CHUNK), CHUNK), z * nx : (z + 1) * nx] = turned[
-                    q * CHUNK : (q + 1) * CHUNK
-                ]
-
-    def turn_beside(n):
-        for c in range(n * ch // len(chips), (n + 1) * ch // len(chips)):
-            turn(c)
+    def shift(z, _):
+        turned = [hbuf[c, z].T for c in range(ch)]
+        for q in range(chunks):
+            lanes = jnp.concatenate([t[q * CHUNK : (q + 1) * CHUNK] for t in turned], axis=0).T.astype(F32)
+            for dx in (-1, 0, 1):
+                rolled = (lanes if dx == 0 else pltpu.roll(lanes, -dx % nx, 0)).astype(BF16)
+                for h in range(halves):
+                    shifted[
+                        h, q, pl.ds(pl.multiple_of(z * part, part), part), (dx + 1) * wide_n : (dx + 2) * wide_n
+                    ] = rolled[h * part : (h + 1) * part]
+        return 0
+
+    def turn_field(h):
+        for p in range(depth + 2):
+            if part % 128 == 0:
+                turned, at, ft = recv_b[h][:, p].astype(F32).reshape(part, ny).astype(BF16).T, p * part, r["ft0"]
+            elif p <= depth:
+                two = [recv_b[h][:, p + i].astype(F32).reshape(part, ny) for i in range(2)]
+                turned = jnp.concatenate(two, axis=0).astype(BF16).T
+                at, ft = (p - p % 2) * part, r["ft%d" % (p % 2)]
+            else:
+                continue
+            at = slice(at, at + turned.shape[1])
+            ft[EDGE : EDGE + ny, at] = turned
+            ft[0:EDGE, at] = turned[ny - EDGE : ny]
+            ft[EDGE + ny : EDGE + ny + EDGE, at] = turned[0:EDGE]
+
+    def planes_from(p, q):
+        odd = 0 if part % 128 == 0 else p % 2
+        return r["ft%d" % odd][q * CHUNK : q * CHUNK + window, (p - odd) * part : (p - odd + depth) * part]
+
+    def part_product(h):
+        turn_field(h)
+        total = None
+        for q in range(chunks):
+            field = jnp.concatenate([planes_from(1 - dz, q) for dz in (-1, 0, 1)], axis=0)
+            term = jnp.dot(field, shifted[h, q], preferred_element_type=F32)
+            total = term if total is None else total + term
+        return total
 
     def fill_taps():
         y_in = lax.broadcasted_iota(jnp.int32, (ny, ny), 0)
@@ -268,9 +293,9 @@
 
     fill_taps()
     h_copy.wait()
+    lax.fori_loop(0, depth // 2, shift, 0)
     order = list(enumerate(chips))
-    merge_send(0, order[:-1], turn_beside)
-    turn_beside(len(chips) - 1)
+    merge_send(0, order[:-1])
     for h in range(1, halves):
         merge_send(h, order[:-1])
     for h in range(halves):
@@ -280,44 +305,30 @@
         turn_send(h)
     wait_a(halves - 1)
     turn_send(halves - 1)
-    for h in range(halves):
+    lax.fori_loop(depth // 2, depth, shift, 0)
+    for h in range(halves - 1):
         wait_b(h)
+        product[...] = part_product(h) if h == 0 else product[...] + part_product(h)
+    wait_b(halves - 1)
+    sums = part_product(halves - 1)
+    if halves > 1:
+        sums = sums + product[...]
+    sums = sums.reshape(3, window, 3 * wide_n)
 
     def moved(q, dx):
         plane = jnp.concatenate([recv_b[h][:, q].astype(F32).reshape(part, ny) for h in range(halves)], axis=0)
         return (plane if dx == 0 else pltpu.roll(plane, dx % nx, 0)).astype(BF16)
 
-    for q in range(depth + 2):
-        for dx in (-1, 0, 1):
-            turned = moved(q, dx).T
-            at = slice(q * nx, (q + 1) * nx)
-            ft[dx + 1, EDGE : EDGE + ny, at] = turned
-            ft[dx + 1, 0:EDGE, at] = turned[ny - EDGE : ny]
-            ft[dx + 1, EDGE + ny : EDGE + ny + EDGE, at] = turned[0:EDGE]
-
-    product = None
-    for q in range(chunks):
-        field = jnp.concatenate(
-            [
-                ft[dx + 1, q * CHUNK : q * CHUNK + window, (1 - dz) * nx : (1 - dz + depth) * nx]
-                for dz in (-1, 0, 1)
-                for dx in (-1, 0, 1)
-            ],
-            axis=0,
-        )
-        term = lax.dot_general(field, ht[q], NT, preferred_element_type=F32)
-        product = term if product is None else product + term
-    product = product.reshape(9, window, ch * CHUNK)
-    w_row = lax.broadcasted_iota(jnp.int32, (window, ch * CHUNK), 0)
-    w_y = lax.rem(lax.broadcasted_iota(jnp.int32, (window, ch * CHUNK), 1), CHUNK)
+    w_row = lax.broadcasted_iota(jnp.int32, (window, 3 * wide_n), 0)
+    w_y = lax.rem(lax.broadcasted_iota(jnp.int32, (window, 3 * wide_n), 1), CHUNK)
     picks = [w_row == w_y + EDGE - dy for dy in (-1, 0, 1)]
-    sums = [
-        jnp.sum(jnp.where(picks[d], product[j], 0.0), axis=0, keepdims=True) for j in range(9) for d in range(3)
-    ]
-    sums.append(jnp.zeros((5, ch * CHUNK), F32))
-    by_tap = jnp.concatenate(sums, axis=0)
-    by_channel = jnp.sum(by_tap.T.reshape(ch, CHUNK, 32), axis=1)
-    by_channel = jnp.concatenate([by_channel, jnp.zeros((ch, 96), F32)], axis=1)
+    by_tap = []
+    for z in range(3):
+        by_tap += [jnp.sum(jnp.where(pick, sums[z], 0.0), axis=0, keepdims=True) for pick in picks]
+        by_tap.append(jnp.zeros((6 if z < 2 else 11, 3 * wide_n), F32))
+    by_tap = jnp.sum(jnp.concatenate(by_tap, axis=0).T.reshape(3, ch, CHUNK, 32), axis=2)
+    by_tap = jnp.concatenate([by_tap, jnp.zeros((3, ch, 96), F32)], axis=2)
+    by_channel = by_tap[0] + pltpu.roll(by_tap[1], 3, 1) + pltpu.roll(by_tap[2], 6, 1)
     of_four = lax.rem(lax.broadcasted_iota(jnp.int32, (ch, 128), 0), 4)
     packed = jnp.where(of_four == 0, by_channel, 0.0)
     for i in range(1, 4):
@@ -378,8 +389,7 @@
 
 
 def write(grads, terms, out, wg, sem):
-    copies = [pltpu.make_async_copy(terms, wg, sem.at[0])]
-    copies += [pltpu.make_async_copy(grads.at[c], out.at[c], sem.at[c + 1]) for c in range(grads.shape[0])]
+    copies = [pltpu.make_async_copy(terms, wg, sem.at[0]), pltpu.make_async_copy(grads, out, sem.at[1])]
     for copy in copies:
         copy.start()
     for copy in copies:
@@ -430,11 +440,14 @@
         scratch["recv_a%d" % h] = pltpu.VMEM((nz + depth + 2, rows, ny), BF16)
         scratch["send_b%d" % h] = pltpu.VMEM((nslab, depth + 2, rows, ny), BF16)
         scratch["recv_b%d" % h] = pltpu.VMEM((nslab, depth + 2, rows, ny), BF16)
-    scratch["ht"] = pltpu.VMEM((ny // CHUNK, ch * CHUNK, depth * nx), BF16)
+    part = nx // halves
+    scratch["shifted"] = pltpu.VMEM((halves, ny // CHUNK, depth * part, 3 * ch * CHUNK), BF16)
+    scratch["product"] = pltpu.VMEM((3 * (CHUNK + 2 * EDGE), 3 * ch * CHUNK), F32)
     scratch["wide"] = pltpu.VMEM((27, ch, ny), F32)
     scratch["wmat"] = pltpu.VMEM((ch // 2, 9 * ny, 2 * ny), BF16)
     scratch["lmat"] = pltpu.VMEM((depth * nx, 9 * ny), BF16)
-    scratch["ft"] = pltpu.VMEM((3, ny + 2 * EDGE, (depth + 2) * nx), BF16)
+    for n in ("ft0", "ft1"):
+        scratch[n] = pltpu.VMEM((ny + 2 * EDGE, (depth + 2) * part), BF16)
     scratch["msg"] = pltpu.VMEM((ch // 4, 128), F32)
     scratch["terms"] = pltpu.VMEM((nbox * nslab, ch // 4, 128), F32)
     scratch["isem"] = dma((7,))
@@ -467,7 +480,7 @@
         out_shape=(pltpu.HBM(hidden_grad.shape, BF16), pltpu.HBM(weight_grad.shape, F32)),
         in_specs=[vmem, vmem],
         out_specs=(hbm, hbm),
-        scratch_shapes=[dma((ch + 1,))],
+        scratch_shapes=[dma((2,))],
     )(pltpu.with_memory_space_constraint(hidden_grad, pltpu.VMEM), pltpu.with_memory_space_constraint(weight_grad, pltpu.VMEM))
     return hidden_grad.reshape(hidden_field.shape), weight_grad
 

time: 27.1 us -> 26.9 us (level)
  no operation moved by 1% of the time
where the time goes in v5:
time: 26.9 us; the launch traced here: 26.7 us
  Pallas kernels  26.1 us (97%)
  between operations  0.64 us (2%)
    pallas_call x1, Pallas kernels, local(): pl.pallas_call(functools.partial(kernel, nbox, nslab, scale, names), out_...  24.7 us
    pallas_call x1, Pallas kernels, local(): pl.pallas_call(write, out_shape=(pltpu.HBM(hidden_grad.shape, BF16), pltp...  1.34 us

profile of v5, /device:TPU:0, one launch (start us, length us, event | category | flops | bytes accessed | tf_op | source)
XLA Modules:
  0.0 26.7 jit_solution(9266111010173776059)
XLA Ops:
  0.6 24.7 %shard_map.104 = (bf16[8,8,128,128]{3,2,1,0:T(8,128)(2,1)S(1)}, f32[8,27]{1,0:T(8,128)S(1)}) custom-call(s32[8]{0:T(128)} %refs_0_.1, s32[8]{0:T(128)} %refs_1_.1, s32[8]{0:T(128)} %refs_2_.1, s32[8]{0:T(128)} %refs_3_.1, s32[8]{0:T(128)} %refs_4_.1, s32[8]{0:T(128)} %refs_5_.1, f32[8,128,128]{2,1,0:T(8,128)} %refs_6_.1, bf16[8,27]{1,0:T(8,128)(2,1)} %refs_7_.1, ...), custom_call_target="tpu_custom_call" | custom-call | tf_op jit(solution)/shard_map/pallas_call | solution.py:465
  25.4 1.3 %shard_map.105 = (bf16[8,8,128,128]{3,2,1,0:T(8,128)(2,1)}, f32[8,27]{1,0:T(8,128)}) custom-call(bf16[8,8,128,128]{3,2,1,0:T(8,128)(2,1)S(1)} %get-tuple-element.6.grads, f32[8,27]{1,0:T(8,128)S(1)} %get-tuple-element.7.terms), custom_call_target="tpu_custom_call" | custom-call | tf_op jit(solution)/shard_map/pallas_call | solution.py:478

commit v6 on v5

--- a/solution.py
+++ b/solution.py
@@ -35,8 +35,7 @@
     r = dict(zip(names, refs, strict=True))
     cone, weight, hbuf, out, wg = r["cone"], r["weight"], r["hbuf"], r["out"], r["wg"]
     bl, bu, plo, pup, wl, wu = (r[n] for n in ("bl", "bu", "plo", "pup", "wl", "wu"))
-    own, z_up, z_dn = r["own"], r["z_up"], r["z_dn"]
-    from_above, from_below = r["from_above"], r["from_below"]
+    own, to_z, from_z = r["own"], r["to_z"], r["from_z"]
     shifted, wide, wmat, lmat, product = r["shifted"], r["wide"], r["wmat"], r["lmat"], r["product"]
     msg, terms = r["msg"], r["terms"]
 
@@ -51,9 +50,8 @@
     chunks = ny // CHUNK
     window = CHUNK + 2 * EDGE
     wide_n = ch * CHUNK
-    send_a = [r["send_a%d" % h] for h in range(halves)]
+    send_a, send_b = r["send_a"], r["send_b"]
     recv_a = [r["recv_a%d" % h] for h in range(halves)]
-    send_b = [r["send_b%d" % h] for h in range(halves)]
     recv_b = [r["recv_b%d" % h] for h in range(halves)]
 
     smalls = [
@@ -94,8 +92,8 @@
             below_c = jnp.where(bl[i] == g - 1, wl[i].astype(F32) * (1.0 / WDEN), 0.0)
             above_c = jnp.where(bu[i] == g + 1, wu[i].astype(F32) * (1.0 / WDEN), 0.0)
             plane = cone[i, h * part : (h + 1) * part].reshape(nslab, rows, ny)
-            z_up[h, :, i] = (above_c * plane).astype(BF16)
-            z_dn[h, :, i] = (below_c * plane).astype(BF16)
+            to_z[0, h, :, i] = (above_c * plane).astype(BF16)
+            to_z[1, h, :, i] = (below_c * plane).astype(BF16)
 
     def weigh_own(i, _):
         lower = wl[i].astype(F32) * (1.0 / WDEN)
@@ -108,31 +106,23 @@
         return pltpu.make_async_remote_copy(
             src_ref=source,
             dst_ref=target,
-            send_sem=send.at[at],
+            send_sem=send.at[0],
             recv_sem=recv.at[at],
             device_id={"slab": me},
             device_id_type=MESH,
         )
 
-    def up_copy(h, c):
+    def z_copy(way, h, c):
         return pltpu.make_async_remote_copy(
-            src_ref=z_up.at[h, pl.ds(2 * c, 2)],
-            dst_ref=from_below.at[h, pl.ds(2 * c, 2)],
-            send_sem=r["up_s"].at[0],
-            recv_sem=r["up_r"].at[h, c],
-            device_id={"box": lax.rem(g + 1, nbox)},
+            src_ref=to_z.at[way, h, pl.ds(2 * c, 2)],
+            dst_ref=from_z.at[h, c, way],
+            send_sem=r["z_s"].at[0],
+            recv_sem=r["z_r"].at[h, c],
+            device_id={"box": lax.rem(g + (1 if way == 0 else nbox - 1), nbox)},
             device_id_type=MESH,
         )
 
-    def dn_copy(h, c):
-        return pltpu.make_async_remote_copy(
-            src_ref=z_dn.at[h, pl.ds(2 * c, 2)],
-            dst_ref=from_above.at[h, pl.ds(2 * c, 2)],
-            send_sem=r["dn_s"].at[0],
-            recv_sem=r["dn_r"].at[h, c],
-            device_id={"box": lax.rem(g + nbox - 1, nbox)},
-            device_id_type=MESH,
-        )
+    inner = jnp.logical_and(g > 0, g < nbox - 1)
 
     chips = [other(lax.div(me, 2), j, nslab // 2) for j in reversed(range(nslab // 2))]
 
@@ -141,17 +131,17 @@
 
             @pl.when(g < nbox - 1)
             def _():
-                up_copy(h, c).start()
+                z_copy(0, h, c).start()
 
             @pl.when(g > 0)
             def _():
-                dn_copy(h, c).start()
+                z_copy(1, h, c).start()
 
     def a_copy(h, t, source):
         return pltpu.make_async_remote_copy(
-            src_ref=send_a[h].at[t],
+            src_ref=send_a.at[h, t],
             dst_ref=recv_a[h].at[pl.ds(source * depth, depth)],
-            send_sem=r["a_s"].at[h],
+            send_sem=r["a_s"].at[0],
             recv_sem=r["a_r"].at[h],
             device_id={"slab": t},
             device_id_type=MESH,
@@ -161,32 +151,36 @@
         sibling = other(me, 1, nslab)
         for n, c in which:
 
-            @pl.when(g < nbox - 1)
+            both = from_z.at[h, c]
+
+            @pl.when(inner)
             def _():
-                dn_copy(h, c).wait_recv()
-
-            @pl.when(g > 0)
+                every(both, both, r["z_s"], r["z_r"], (h, c)).wait_recv()
+
+            @pl.when(jnp.logical_not(inner))
             def _():
-                up_copy(h, c).wait_recv()
-
-            def merged(t):
-                return (own[h, t] + from_above[h, t].astype(F32) + from_below[h, t].astype(F32)).astype(BF16)
-
-            last = n == len(chips) - 1
-            for t in (sibling, me) if last else (2 * c, 2 * c + 1):
-                if last and t is me:
-                    recv_a[h][pl.ds(me * depth, depth)] = merged(me)
-                else:
-                    send_a[h][t] = merged(t)
-                    a_copy(h, t, me).start()
+                every(both.at[0], both.at[0], r["z_s"], r["z_r"], (h, c)).wait_recv()
+
+            def merged(t, at):
+                moved_in = from_z[h, c, 0, at].astype(F32) + from_z[h, c, 1, at].astype(F32)
+                return (own[h, t] + moved_in).astype(BF16)
+
+            if n < len(chips) - 1:
+                for i in range(2):
+                    send_a[h, 2 * c + i] = merged(2 * c + i, i)
+                    a_copy(h, 2 * c + i, me).start()
+            else:
+                send_a[h, sibling] = merged(sibling, sibling - 2 * c)
+                a_copy(h, sibling, me).start()
+                recv_a[h][pl.ds(me * depth, depth)] = merged(me, me - 2 * c)
     def wait_a(h):
-        every(send_a[h].at[: nslab - 1], recv_a[h].at[: (nslab - 1) * depth], r["a_s"], r["a_r"], h).wait_recv()
+        every(send_a.at[h, : nslab - 1], recv_a[h].at[: (nslab - 1) * depth], r["a_s"], r["a_r"], h).wait_recv()
 
     def b_copy(h, s, source):
         return pltpu.make_async_remote_copy(
-            src_ref=send_b[h].at[s],
+            src_ref=send_b.at[h, s],
             dst_ref=recv_b[h].at[source],
-            send_sem=r["b_s"].at[h],
+            send_sem=r["b_s"].at[0],
             recv_sem=r["b_r"].at[h],
             device_id={"slab": s},
             device_id_type=MESH,
@@ -202,12 +196,12 @@
 
         for j in reversed(range(1, nslab)):
             s = other(me, j, nslab)
-            send_b[h][s] = wanted(s)
+            send_b[h, s] = wanted(s)
             b_copy(h, s, me).start()
         recv_b[h][me] = wanted(me)
 
     def wait_b(h):
-        every(send_b[h].at[: nslab - 1], recv_b[h].at[: nslab - 1], r["b_s"], r["b_r"], h).wait_recv()
+        every(send_b.at[h, : nslab - 1], recv_b[h].at[: nslab - 1], r["b_s"], r["b_r"], h).wait_recv()
 
     def shift(z, _):
         turned = [hbuf[c, z].T for c in range(ch)]
@@ -285,11 +279,11 @@
 
     @pl.when(g == nbox - 1)
     def _():
-        from_above[...] = jnp.zeros_like(from_above)
+        from_z[:, :, 1] = jnp.zeros_like(from_z[:, :, 1])
 
     @pl.when(g == 0)
     def _():
-        from_below[...] = jnp.zeros_like(from_below)
+        from_z[:, :, 0] = jnp.zeros_like(from_z[:, :, 0])
 
     fill_taps()
     h_copy.wait()
@@ -369,17 +363,17 @@
                     lmat[z * nx : (z + 1) * nx, j * ny : (j + 1) * ny] = plane
     lax.fori_loop(0, pairs, pair_grads, 0)
 
-    @pl.when(g < nbox - 1)
+    @pl.when(inner)
     def _():
-        every(z_up, from_below, r["up_s"], r["up_s"], 0).wait_send()
-
-    @pl.when(g > 0)
+        every(to_z, to_z, r["z_s"], r["z_s"], 0).wait_send()
+
+    @pl.when(jnp.logical_not(inner))
     def _():
-        every(z_dn, from_above, r["dn_s"], r["dn_s"], 0).wait_send()
-
-    for h in range(halves):
-        every(send_a[h].at[: nslab - 1], recv_a[h].at[: (nslab - 1) * depth], r["a_s"], r["a_r"], h).wait_send()
-        every(send_b[h].at[: nslab - 1], recv_b[h].at[: nslab - 1], r["b_s"], r["b_r"], h).wait_send()
+        every(to_z.at[0], to_z.at[0], r["z_s"], r["z_s"], 0).wait_send()
+
+    a_sent, b_sent = send_a.at[:, : nslab - 1], send_b.at[:, : nslab - 1]
+    every(a_sent, a_sent, r["a_s"], r["a_s"], 0).wait_send()
+    every(b_sent, b_sent, r["b_s"], r["b_s"], 0).wait_send()
     r_all = every(terms.at[: ndev - 1], terms.at[: ndev - 1], r["r_s"], r["r_r"], 0)
     r_all.wait_send()
     r_all.wait_recv()
@@ -433,12 +427,12 @@
     scratch["weight"] = pltpu.VMEM(conv_weight.shape, BF16)
     scratch["hbuf"] = pltpu.VMEM((ch, depth, nx, ny), BF16)
     scratch["own"] = pltpu.VMEM(chunk, F32)
-    for n in ("z_up", "z_dn", "from_above", "from_below"):
-        scratch[n] = pltpu.VMEM(chunk, BF16)
+    scratch["to_z"] = pltpu.VMEM((2, *chunk), BF16)
+    scratch["from_z"] = pltpu.VMEM((halves, nslab // 2, 2, 2, depth, rows, ny), BF16)
+    scratch["send_a"] = pltpu.VMEM(chunk, BF16)
+    scratch["send_b"] = pltpu.VMEM((halves, nslab, depth + 2, rows, ny), BF16)
     for h in range(halves):
-        scratch["send_a%d" % h] = pltpu.VMEM(chunk[1:], BF16)
         scratch["recv_a%d" % h] = pltpu.VMEM((nz + depth + 2, rows, ny), BF16)
-        scratch["send_b%d" % h] = pltpu.VMEM((nslab, depth + 2, rows, ny), BF16)
         scratch["recv_b%d" % h] = pltpu.VMEM((nslab, depth + 2, rows, ny), BF16)
     part = nx // halves
     scratch["shifted"] = pltpu.VMEM((halves, ny // CHUNK, depth * part, 3 * ch * CHUNK), BF16)
@@ -453,11 +447,10 @@
     scratch["isem"] = dma((7,))
     scratch["csem"] = dma((halves,))
     scratch["hsem"] = dma((1,))
-    for n in ("up", "dn"):
+    scratch["z_s"] = dma((1,))
+    scratch["z_r"] = dma((halves, nslab // 2))
+    for n in ("a", "b"):
         scratch[n + "_s"] = dma((1,))
-        scratch[n + "_r"] = dma((halves, nslab // 2))
-    for n in ("a", "b"):
-        scratch[n + "_s"] = dma((halves,))
         scratch[n + "_r"] = dma((halves,))
     scratch["r_s"] = dma((1,))
     scratch["r_r"] = dma((1,))

time: 26.9 us -> 26.8 us (level)
  no operation moved by 1% of the time
where the time goes in v6:
time: 26.8 us; the launch traced here: 26.6 us
  Pallas kernels  26 us (97%)
  between operations  0.64 us (2%)
    pallas_call x1, Pallas kernels, local(): pl.pallas_call(functools.partial(kernel, nbox, nslab, scale, names), out_...  24.6 us
    pallas_call x1, Pallas kernels, local(): pl.pallas_call(write, out_shape=(pltpu.HBM(hidden_grad.shape, BF16), pltp...  1.34 us

profile of v6, /device:TPU:0, one launch (start us, length us, event | category | flops | bytes accessed | tf_op | source)
XLA Modules:
  0.0 26.6 jit_solution(8493388914240983810)
XLA Ops:
  0.6 24.6 %shard_map.104 = (bf16[8,8,128,128]{3,2,1,0:T(8,128)(2,1)S(1)}, f32[8,27]{1,0:T(8,128)S(1)}) custom-call(s32[8]{0:T(128)} %refs_0_.1, s32[8]{0:T(128)} %refs_1_.1, s32[8]{0:T(128)} %refs_2_.1, s32[8]{0:T(128)} %refs_3_.1, s32[8]{0:T(128)} %refs_4_.1, s32[8]{0:T(128)} %refs_5_.1, f32[8,128,128]{2,1,0:T(8,128)} %refs_6_.1, bf16[8,27]{1,0:T(8,128)(2,1)} %refs_7_.1, ...), custom_call_target="tpu_custom_call" | custom-call | tf_op jit(solution)/shard_map/pallas_call | solution.py:458
  25.3 1.3 %shard_map.105 = (bf16[8,8,128,128]{3,2,1,0:T(8,128)(2,1)}, f32[8,27]{1,0:T(8,128)}) custom-call(bf16[8,8,128,128]{3,2,1,0:T(8,128)(2,1)S(1)} %get-tuple-element.6.grads, f32[8,27]{1,0:T(8,128)S(1)} %get-tuple-element.7.terms), custom_call_target="tpu_custom_call" | custom-call | tf_op jit(solution)/shard_map/pallas_call | solution.py:471

commit v7 on v6

--- a/solution.py
+++ b/solution.py
@@ -194,7 +194,7 @@
         def wanted(s):
             return recv_a[h][pl.ds(lax.rem(s * depth - 1 - offset + 2 * nz, nz), depth + 2)]
 
-        for j in reversed(range(1, nslab)):
+        for j in sorted(range(1, nslab), key=lambda j: (-(j // 2).bit_count(), j % 2, j)):
             s = other(me, j, nslab)
             send_b[h, s] = wanted(s)
             b_copy(h, s, me).start()

time: 26.8 us -> 26.7 us (level)
  no operation moved by 1% of the time
where the time goes in v7:
time: 26.7 us; the launch traced here: 26.6 us
  Pallas kernels  25.9 us (97%)
  between operations  0.64 us (2%)
    pallas_call x1, Pallas kernels, local(): pl.pallas_call(functools.partial(kernel, nbox, nslab, scale, names), out_...  24.6 us
    pallas_call x1, Pallas kernels, local(): pl.pallas_call(write, out_shape=(pltpu.HBM(hidden_grad.shape, BF16), pltp...  1.34 us

profile of v7, /device:TPU:0, one launch (start us, length us, event | category | flops | bytes accessed | tf_op | source)
XLA Modules:
  0.0 26.6 jit_solution(7057810935006726828)
XLA Ops:
  0.6 24.6 %shard_map.104 = (bf16[8,8,128,128]{3,2,1,0:T(8,128)(2,1)S(1)}, f32[8,27]{1,0:T(8,128)S(1)}) custom-call(s32[8]{0:T(128)} %refs_0_.1, s32[8]{0:T(128)} %refs_1_.1, s32[8]{0:T(128)} %refs_2_.1, s32[8]{0:T(128)} %refs_3_.1, s32[8]{0:T(128)} %refs_4_.1, s32[8]{0:T(128)} %refs_5_.1, f32[8,128,128]{2,1,0:T(8,128)} %refs_6_.1, bf16[8,27]{1,0:T(8,128)(2,1)} %refs_7_.1, ...), custom_call_target="tpu_custom_call" | custom-call | tf_op jit(solution)/shard_map/pallas_call | solution.py:458
  25.2 1.3 %shard_map.105 = (bf16[8,8,128,128]{3,2,1,0:T(8,128)(2,1)}, f32[8,27]{1,0:T(8,128)}) custom-call(bf16[8,8,128,128]{3,2,1,0:T(8,128)(2,1)S(1)} %get-tuple-element.6.grads, f32[8,27]{1,0:T(8,128)S(1)} %get-tuple-element.7.terms), custom_call_target="tpu_custom_call" | custom-call | tf_op jit(solution)/shard_map/pallas_call | solution.py:471
